TPU v7x, 512 devices: a whole 4x4x16 slice. The times are simulated.
512 devices in a mesh: dp: 64 (over z, x), tensor: 8 (over y, core).
Axes of the slice: x: 4, y: 4, z: 16, core: 2. Of those that a mesh axis runs over, the one named last changes fastest.
Arguments:
- query_rows: bfloat16 [16384, 8192], P('dp', 'tensor'), may hold values from -7.5 to 7.5
- key_rows: bfloat16 [16384, 1024], P('dp', 'tensor'), may hold values from -7.5 to 7.5
- value_rows: bfloat16 [16384, 1024], P('dp', 'tensor'), may hold values from -6 to 6
- output_grad: bfloat16 [16384, 8192], P('dp', 'tensor'), may hold values from -6 to 6
- layer_input: bfloat16 [16384, 8192], P('dp', 'tensor'), may hold values from -16 to 16
- token_document: int32 [16384], P('dp'), may hold values from 0 to 255, as said below
- token_offset: int32 [16384], P('dp'), may hold values from 0 to 487, as said below
- document_server: int32 [256], replicated, may hold values from 0 to 63, as said below
Outputs:
- attended: bfloat16 [16384, 8192], P('dp', 'tensor')
- query_grad: bfloat16 [16384, 8192], P('dp', 'tensor')
- key_grad: bfloat16 [16384, 1024], P('dp', 'tensor')
- value_grad: bfloat16 [16384, 1024], P('dp', 'tensor')
- weight_grad: float32 [8192, 1024], P(('tensor', 'dp'))
Inputs may be any that keep to these rules, and one draw needn't show every extreme that they name: `token_document`: token t sits on dp index t // 256. The rows of a dp index come in aligned runs of 8 rows, each run one piece of one document. At most 8 tokens of one dp index belong to the documents of one server, and in every draw some server has exactly 8 tokens from every dp index. Every document has at least one token. `token_offset`: within a piece the offsets are consecutive and rising, starting at a multiple of 8; the offsets of one document's tokens are 0 up to its length minus one, each once. `document_server`: each server is named by exactly 4 documents.
All inputs are finite; a program needn't handle non-finite values.
Results may differ from a plain program's by a relative error of at most 0.008.
The roundings to bfloat16 on the way count: a program that leaves them out, or rounds other values in their place, can miss the bound.
Values may be sent and summed in bfloat16 or wider, within the bound.
No kernel may reach another device: no remote copies, remote signals or barrier semaphores. Data moves between devices by JAX's collectives and lax.ppermute only.
A program may use at most 64 MiB of HBM per device.

v0:
```python
import math

import jax
import jax.numpy as jnp
from jax import lax
from jax.sharding import PartitionSpec as P

HD = 128


NEG_FILL = -1e30


def pick(block, index):
    return lax.dynamic_slice_in_dim(block, index * HD, HD, 1)


def add_at(block, index, part):
    return pick(block, index) + part


def merge_heads(stacked):
    return jnp.transpose(stacked, (1, 0, 2)).reshape(stacked.shape[1], -1)


def head_scores(query_head, key_head, allowed):
    scale = float(HD) ** (-0.5)
    scores = jnp.dot(query_head, key_head.T, preferred_element_type=jnp.float32) * scale
    return jnp.where(allowed, scores, NEG_FILL)


def softmax_parts(scores):
    row_max = jnp.max(scores, axis=1, keepdims=True)
    exp_scores = jnp.exp(scores - row_max)
    row_total = jnp.sum(exp_scores, axis=1, keepdims=True)
    return (exp_scores / row_total, row_max, row_total)


def head_backward(weights, weights_low, row_delta, query_head, key_head, value_head, grad_head):
    scale = float(HD) ** (-0.5)
    grad_weights = jnp.dot(grad_head, value_head.T, preferred_element_type=jnp.float32)
    grad_scores = (weights * (grad_weights - row_delta)).astype(jnp.bfloat16)
    query_grad = jnp.dot(grad_scores, key_head, preferred_element_type=jnp.float32) * scale
    key_grad = jnp.dot(grad_scores.T, query_head, preferred_element_type=jnp.float32) * scale
    value_grad = jnp.dot(weights_low.T, grad_head, preferred_element_type=jnp.float32)
    return (query_grad, key_grad, value_grad)


def joint_pass(query_block, key_block, value_block, grad_block, allowed):
    slot_count = query_block.shape[0]
    query_heads = query_block.shape[1] // HD
    group = query_heads // (key_block.shape[1] // HD)

    def one_head(carry, head):
        key_acc, value_acc = carry
        kv_head = head // group
        query_head = pick(query_block, head)
        key_head = pick(key_block, kv_head)
        value_head = pick(value_block, kv_head)
        grad_head = pick(grad_block, head)
        weights, row_max, row_total = softmax_parts(head_scores(query_head, key_head, allowed))
        weights_low = weights.astype(jnp.bfloat16)
        mixed_full = jnp.dot(weights_low, value_head, preferred_element_type=jnp.float32)
        row_delta = jnp.sum(grad_head.astype(jnp.float32) * mixed_full, axis=1, keepdims=True)
        query_grad, key_grad, value_grad = head_backward(
            weights, weights_low, row_delta, query_head, key_head, value_head, grad_head
        )
        key_acc = add_at(key_acc, kv_head, key_grad)
        value_acc = add_at(value_acc, kv_head, value_grad)
        return (
            (key_acc, value_acc),
            (mixed_full.astype(jnp.bfloat16), query_grad.astype(jnp.bfloat16)),
        )

    empty = jnp.zeros((slot_count, key_block.shape[1]), jnp.float32)
    (key_acc, value_acc), (mixed, query_grad) = lax.scan(
        one_head, (empty, empty), jnp.arange(query_heads, dtype=jnp.int32)
    )
    return (
        merge_heads(mixed),
        merge_heads(query_grad),
        key_acc.astype(jnp.bfloat16),
        value_acc.astype(jnp.bfloat16),
    )


def shards(
    query_rows,
    key_rows,
    value_rows,
    output_grad,
    layer_input,
    token_document,
    token_offset,
    document_server,
):
    dp_size = lax.axis_size("dp")
    tok_dev = query_rows.shape[0]
    capacity = 2 * tok_dev // dp_size
    slot_count = dp_size * capacity
    query_width = query_rows.shape[1]
    kv_width = key_rows.shape[1]
    document_ids = jnp.arange(document_server.shape[0], dtype=jnp.int32)
    own_server = jnp.sum(
        jnp.where(token_document[..., None] == document_ids, document_server, 0), axis=-1
    )
    member = (own_server[:, None] == jnp.arange(dp_size, dtype=jnp.int32)[None, :]).astype(
        jnp.int32
    )
    order_rank = jnp.sum((jnp.cumsum(member, axis=0) - member) * member, axis=1)
    slot_index = own_server * capacity + order_rank
    token_ids = jnp.arange(tok_dev, dtype=jnp.int32)
    source_token = jnp.zeros((slot_count,), jnp.int32).at[slot_index].set(token_ids)
    occupied = jnp.zeros((slot_count,), jnp.int32).at[slot_index].set(1) > 0
    payload = jnp.concatenate([query_rows, key_rows, value_rows, output_grad], axis=1)
    sent = jnp.where(
        occupied[:, None], jnp.take(payload, source_token, axis=0), jnp.zeros((), payload.dtype)
    )
    arrived = lax.all_to_all(
        sent.reshape(dp_size, capacity, -1), "dp", split_axis=0, concat_axis=0, tiled=True
    ).reshape(slot_count, -1)
    tag_rows = jnp.stack(
        [
            jnp.where(occupied, jnp.take(token_document, source_token), -1),
            jnp.where(occupied, jnp.take(token_offset, source_token), -1),
        ],
        axis=1,
    )
    arrived_tags = lax.all_to_all(
        tag_rows.reshape(dp_size, capacity, 2), "dp", split_axis=0, concat_axis=0, tiled=True
    ).reshape(slot_count, 2)
    slot_document = arrived_tags[:, 0]
    slot_position = arrived_tags[:, 1]
    allowed = (slot_document[:, None] == slot_document[None, :]) & (
        slot_position[None, :] <= slot_position[:, None]
    )
    query_block = arrived[:, :query_width]
    key_block = arrived[:, query_width : query_width + kv_width]
    value_block = arrived[:, query_width + kv_width : query_width + 2 * kv_width]
    served = joint_pass(
        query_block, key_block, value_block, arrived[:, query_width + 2 * kv_width :], allowed
    )
    results = jnp.concatenate(list(served), axis=1)
    returned = lax.all_to_all(
        results.reshape(dp_size, capacity, -1), "dp", split_axis=0, concat_axis=0, tiled=True
    ).reshape(slot_count, -1)
    own_rows = jnp.take(returned, slot_index, axis=0)
    attended = own_rows[:, :query_width]
    query_grad = own_rows[:, query_width : 2 * query_width]
    key_grad = own_rows[:, 2 * query_width : 2 * query_width + kv_width]
    value_grad = own_rows[:, 2 * query_width + kv_width :]
    all_value_grads = lax.all_gather(value_grad, "tensor", axis=1, tiled=True)
    weight_grad = lax.psum_scatter(
        lax.dot_general(
            layer_input,
            all_value_grads,
            (((0,), (0,)), ((), ())),
            preferred_element_type=jnp.float32,
        ),
        "dp",
        scatter_dimension=0,
        tiled=True,
    ) * (1.0 / math.sqrt(tok_dev * dp_size))
    return (attended, query_grad, key_grad, value_grad, weight_grad)


def solution(mesh):
    return jax.shard_map(
        shards,
        mesh=mesh,
        in_specs=(
            P("dp", "tensor"),
            P("dp", "tensor"),
            P("dp", "tensor"),
            P("dp", "tensor"),
            P("dp", "tensor"),
            P("dp"),
            P("dp"),
            P(),
        ),
        out_specs=(
            P("dp", "tensor"),
            P("dp", "tensor"),
            P("dp", "tensor"),
            P("dp", "tensor"),
            P(("tensor", "dp"), None),
        ),
        check_vma=False,
    )
```

profile of v0, /device:TPU:8, one launch (start us, length us, event | category | flops | bytes accessed | tf_op | source)
XLA Modules:
  0.0 1087.8 jit_solution(16913046313422714264)
XLA Ops:
  9.1 1.4 scatter_custom_fusion.1
  10.6 1.4 scatter_custom_fusion
  12.0 3.6 gather_fusion.2
  15.6 3.5 gather_fusion.3
  20.1 18.6 %all-to-all-start.1 = ((s32[64,8,2]{1,2,0:T(2,128)}), s32[64,8,2]{1,2,0:T(2,128)S(1)}, u32[]{:S(2)}, u32[]{:S(2)}) async-start(s32[64,8,2]{1,2,0:T(2,128)} %copy.45), calls=%async_computation.1 | async-start | bytes 131072 | tf_op jit(solution)/shard_map/all_to_all | solution.py:129
  39.0 3.4 gather_fusion
  42.4 3.4 fusion.16
  45.8 8.0 all-to-all-done.1
  53.8 7.1 all-to-all-start
  61.1 110.7 %all-to-all-done = bf16[64,8,2304]{2,1,0:T(8,128)(2,1)S(1)} async-done(((bf16[64,8,2304]{2,1,0:T(8,128)(2,1)}), bf16[64,8,2304]{2,1,0:T(8,128)(2,1)S(1)}, u32[]{:S(2)}, u32[]{:S(2)}) %all-to-all-start) | async-done | bytes 2359328 | tf_op jit(solution)/shard_map/all_to_all | solution.py:119
  172.5 1.6 fusion.27
  174.1 63.3 %while.17 = (s32[]{:T(128)}, f32[512,128]{1,0:T(8,128)S(1)}, f32[512,128]{1,0:T(8,128)S(1)}, bf16[8,512,128]{1,2,0:T(8,128)(2,1)}, bf16[8,512,128]{2,1,0:T(8,128...) while((s32[]{:T(128)}, f32[512,128]{1,0:T(8,128)S(1)}, ...), condition=%wide.region_10.12_spmd.clone, body=%wide.region_6.11_spmd.clone.sunk | while | flops 407566848 | bytes 11168018 | solution.py:76
  192.3 1.4 fusion.71
  237.5 1.9 copy.50
  239.9 1.7 copy.49
  242.9 2.8 pad_maximum_fusion
  245.7 6.0 all-to-all-start.2
  251.8 110.5 %all-to-all-done.2 = bf16[64,8,2304]{2,1,0:T(8,128)(2,1)S(1)} async-done(((bf16[64,8,2304]{2,1,0:T(8,128)(2,1)}), bf16[64,8,2304]{2,1,0:T(8,128)(2,1)S(1)}, u32[]{:S(2)}, u32[]{:S(2)}) %all-to-all-start.2) | async-done | bytes 2359328 | tf_op jit(solution)/shard_map/all_to_all | solution.py:144
  362.3 2.4 gather_fusion.1
  364.7 1.4 broadcast_select_fusion
  366.8 13.1 %all_gather.3 = bf16[256,1024]{1,0:T(8,128)(2,1)S(1)} all-gather(bf16[256,128]{1,0:T(8,128)(2,1)S(1)} %get-tuple-element.235), channel_id=1, replica_groups=mesh['dp'=64,'tensor'=8] {'tensor'}, dimensions={1}, use_global_device_ids=true | all-gather | bytes 589824 | tf_op jit(solution)/shard_map/all_gather | solution.py:152
  379.9 2.7 convolution_bitcast_fusion
  382.6 5.3 copy.53
  389.1 689.9 %reduce-scatter.4.cloned.1.call-done = f32[16,1024]{1,0:T(8,128)} async-done(((f32[1024,1024]{1,0:T(8,128)}), f32[16,1024]{1,0:T(8,128)}) %reduce-scatter.4.cloned.1.call-update) | async-done | bytes 65552
  (167 shorter events, 65.6 us)
Async XLA Ops:
  7.2 372.7 %copy-start = (bf16[256,1024]{1,0:T(8,128)(2,1)S(1)}, bf16[256,1024]{1,0:T(8,128)(2,1)}, u32[]{:S(2)}) copy-start(bf16[256,1024]{1,0:T(8,128)(2,1)} %param.16) | copy-start | bytes 1572868
  7.2 8.5 copy-start.1
  10.5 28.3 %copy-start.3 = (bf16[256,1024]{1,0:T(8,128)(2,1)S(1)}, bf16[256,1024]{1,0:T(8,128)(2,1)}, u32[]{:S(2)}) copy-start(bf16[256,1024]{1,0:T(8,128)(2,1)} %param.15) | copy-start | bytes 1572868
  10.5 28.3 %copy-start.4 = (bf16[256,1024]{1,0:T(8,128)(2,1)S(1)}, bf16[256,1024]{1,0:T(8,128)(2,1)}, u32[]{:S(2)}) copy-start(bf16[256,1024]{1,0:T(8,128)(2,1)} %param.12) | copy-start | bytes 1572868
  10.6 28.3 %copy-start.6 = (bf16[256,128]{1,0:T(8,128)(2,1)S(1)}, bf16[256,128]{1,0:T(8,128)(2,1)}, u32[]{:S(2)}) copy-start(bf16[256,128]{1,0:T(8,128)(2,1)} %param.14) | copy-start | bytes 196612
  10.6 28.3 %copy-start.7 = (bf16[256,128]{1,0:T(8,128)(2,1)S(1)}, bf16[256,128]{1,0:T(8,128)(2,1)}, u32[]{:S(2)}) copy-start(bf16[256,128]{1,0:T(8,128)(2,1)} %param.13) | copy-start | bytes 196612
  20.1 33.8 %all-to-all-start.1 = ((s32[64,8,2]{1,2,0:T(2,128)}), s32[64,8,2]{1,2,0:T(2,128)S(1)}, u32[]{:S(2)}, u32[]{:S(2)}) async-start(s32[64,8,2]{1,2,0:T(2,128)} %copy.45), calls=%async_computation.1 | async-start | bytes 131072 | tf_op jit(solution)/shard_map/all_to_all | solution.py:129
  53.8 118.0 %all-to-all-start = ((bf16[64,8,2304]{2,1,0:T(8,128)(2,1)}), bf16[64,8,2304]{2,1,0:T(8,128)(2,1)S(1)}, u32[]{:S(2)}, u32[]{:S(2)}) async-start(bf16[64,8,2304]{2,1,0:T(8,128)(2,1)} %fusion.16), calls=%async_computation | async-start | bytes 4718592 | tf_op jit(solution)/shard_map/all_to_all | solution.py:119
  178.8 1.6 copy-start.2
  186.7 1.6 copy-start.2
  194.6 1.6 copy-start.2
  202.5 1.6 copy-start.2
  210.5 1.6 copy-start.2
  218.4 1.6 copy-start.2
  226.3 1.6 copy-start.2
  234.2 1.6 copy-start.2
  245.7 116.5 %all-to-all-start.2 = ((bf16[64,8,2304]{2,1,0:T(8,128)(2,1)}), bf16[64,8,2304]{2,1,0:T(8,128)(2,1)S(1)}, u32[]{:S(2)}, u32[]{:S(2)}) async-start(bf16[64,8,2304]{2,1,0:T(8,128)(2,1)} %pad_maximum_fusion), calls=%async_computation.2 | async-start | bytes 4718592 | tf_op jit(solution)/shard_map/all_to_all | solution.py:144
  251.8 827.3 %reduce-scatter.4.cloned.1.call-start = ((), (), s32[]{:S(2)}) async-start(), calls=%async_computation.4 | async-start | bytes 4259840
  366.8 15.8 %copy-start.5 = (bf16[256,128]{1,0:T(8,128)(2,1)}, bf16[256,128]{1,0:T(8,128)(2,1)S(1)}, u32[]{:S(2)}) copy-start(bf16[256,128]{1,0:T(8,128)(2,1)S(1)} %get-tuple-element.235) | copy-start | bytes 196612
Sparse Core Ops, SparseCore 0:
  388.1 690.8 reduce-scatter.3
where the time goes:
time: 1090 us
  waiting for transfers between devices  919 us (84%)
  local copies, waits for them, and re-layouts  52 us (5%)
  matrix products  39.1 us (4%)
  starting transfers between devices  31.7 us (3%)
  between operations  14.4 us (1%)
  blocking collectives  13.1 us (1%)
  other arithmetic  12.5 us (1%)
    unnamed x2, waiting for transfers between devices  690 us
    all_to_all x1, waiting for transfers between devices, shards(): lax.all_to_all(sent.reshape(dp_size, capacity, -1), 'dp', split_axis=0, c...  111 us
    all_to_all x1, waiting for transfers between devices, shards(): lax.all_to_all(results.reshape(dp_size, capacity, -1), 'dp', split_axis=0...  110 us
  transfers between devices with their start and end apart: 4, of which 4 were waited for; matrix products, arithmetic and copies ran while one was open for 1% of the time, Pallas kernels for 0%

commit v1 on v0

v1 whole, which is shorter than its diff:
```python
import functools
import math

import jax
import jax.numpy as jnp
from jax import lax
from jax.experimental import pallas as pl
from jax.experimental.pallas import tpu as pltpu
from jax.sharding import Mesh
from jax.sharding import PartitionSpec as P

HD = 128
RUN = 8
X_SIZE = 4
MAX_RUNS = 64
NEG_FILL = -1e30
F32 = jnp.float32
BF16 = jnp.bfloat16
NT = (((1,), (1,)), ((), ()))
DP = ("z", "x")


def whole(memory=pltpu.VMEM):
    return pl.BlockSpec(memory_space=memory)


def params():
    return pltpu.CompilerParams(vmem_limit_bytes=50 * 1024 * 1024)


def pack_kernel(slot_ref, query_ref, grad_ref, key_ref, value_ref, out_ref):
    slots, tokens = out_ref.shape[0], slot_ref.shape[1]
    ids = lax.broadcasted_iota(jnp.int32, (slots, tokens), 0)
    hot = (ids == slot_ref[...]).astype(F32).astype(BF16)
    at = 0
    for ref in (query_ref, grad_ref, key_ref, value_ref):
        width = ref.shape[1]
        out_ref[:, at : at + width] = jnp.dot(hot, ref[...], preferred_element_type=F32).astype(BF16)
        at += width


def turn_kernel(per_z, layer_ref, out_ref):
    width = layer_ref.shape[1]
    rows = width // X_SIZE
    for x in range(X_SIZE):
        new = lax.broadcasted_iota(jnp.int32, (rows, width), 0)
        old = lax.broadcasted_iota(jnp.int32, (rows, width), 1)
        source = (new // per_z) * (per_z * X_SIZE) + x * per_z + new % per_z
        hot = (source == old).astype(F32).astype(BF16)
        out_ref[x] = lax.dot_general(hot, layer_ref[...], NT, preferred_element_type=F32).astype(BF16)


def server_kernel(group, row_doc, row_pos, col_doc, col_pos, query_ref, grad_ref, key_ref, value_ref, out_ref, bias, key_acc, value_acc):
    head = pl.program_id(0)

    @pl.when(head == 0)
    def _():
        allowed = (row_doc[...] == col_doc[...]) & (row_pos[...] <= col_pos[...])
        bias[...] = jnp.where(allowed, 0.0, NEG_FILL)
        key_acc[...] = jnp.zeros_like(key_acc)
        value_acc[...] = jnp.zeros_like(value_acc)

    scale = float(HD) ** (-0.5)
    query, grad = query_ref[...], grad_ref[...]
    scores = lax.dot_general(key_ref[...], query, NT, preferred_element_type=F32) + bias[...]
    top = jnp.max(scores, axis=0, keepdims=True)
    exp_scores = jnp.exp((scores - top) * scale)
    total = jnp.sum(exp_scores, axis=0, keepdims=True)
    weights = exp_scores * (1.0 / total)
    weights_low = weights.astype(BF16)
    grad_weights = lax.dot_general(value_ref[...], grad, NT, preferred_element_type=F32)
    row_delta = jnp.sum(weights_low.astype(F32) * grad_weights, axis=0, keepdims=True)
    grad_scores = (weights * (grad_weights - row_delta)).astype(BF16)
    value_acc[...] += jnp.dot(weights_low, grad, preferred_element_type=F32)
    key_acc[...] += jnp.dot(grad_scores, query, preferred_element_type=F32)

    @pl.when(head == group - 1)
    def _():
        out_ref[:, :HD] = (key_acc[...] * scale).astype(BF16)
        out_ref[:, HD:] = value_acc[...].astype(BF16)


def home_kernel(
    group, unroll, place_ref, reach_ref, query_ref, grad_ref, pairs_ref, mixed_ref, query_grad_ref,
    pairs, rows, query, grad, mixed, query_grad,
):
    scale = float(HD) ** (-0.5)
    count = query_ref.shape[0] // RUN
    reach_rows = rows.shape[1]
    pairs[...] = pairs_ref[...].astype(F32)
    query[...] = query_ref[...].astype(F32)
    grad[...] = grad_ref[...].astype(F32)
    rows[...] = jnp.zeros_like(rows)
    token = lax.broadcasted_iota(jnp.int32, (group * RUN, reach_rows), 0) % RUN
    other = lax.broadcasted_iota(jnp.int32, (group * RUN, reach_rows), 1)

    def stack(ref, run):
        parts = [ref[pl.ds(pl.multiple_of(run * RUN, RUN), RUN), h * HD : (h + 1) * HD] for h in range(group)]
        return jnp.concatenate(parts, axis=0)

    def unstack(ref, run, block):
        for h in range(group):
            ref[pl.ds(pl.multiple_of(run * RUN, RUN), RUN), h * HD : (h + 1) * HD] = block[h * RUN : (h + 1) * RUN]

    def step(index, carry):
        for u in range(unroll):
            run = index * unroll + u

            def bring(k, c, run=run, u=u):
                source = pl.multiple_of(place_ref[run, k] * RUN, RUN)
                rows[u, pl.ds(pl.multiple_of(k * RUN, RUN), RUN), :] = pairs[pl.ds(source, RUN), :]
                return c

            lax.fori_loop(0, reach_ref[run] + 1, bring, 0)
        for u in range(unroll):
            run = index * unroll + u
            block = rows[u].astype(BF16)
            keys, values = block[:, :HD], block[:, HD:]
            query_run = stack(query, run).astype(BF16)
            grad_full = stack(grad, run)
            grad_run = grad_full.astype(BF16)
            scores = lax.dot_general(query_run, keys, NT, preferred_element_type=F32)
            scores = jnp.where(other <= token + reach_ref[run] * RUN, scores, NEG_FILL)
            top = jnp.max(scores, axis=1, keepdims=True)
            exp_scores = jnp.exp((scores - top) * scale)
            total = jnp.sum(exp_scores, axis=1, keepdims=True)
            weights = exp_scores * (1.0 / total)
            mixed_full = jnp.dot(weights.astype(BF16), values, preferred_element_type=F32)
            row_delta = jnp.sum(grad_full * mixed_full, axis=1, keepdims=True)
            grad_weights = lax.dot_general(grad_run, values, NT, preferred_element_type=F32)
            grad_scores = (weights * (grad_weights - row_delta)).astype(BF16)
            unstack(mixed, run, mixed_full)
            unstack(query_grad, run, jnp.dot(grad_scores, keys, preferred_element_type=F32) * scale)
        return carry

    lax.fori_loop(0, count // unroll, step, 0)
    mixed_ref[...] = mixed[...].astype(BF16)
    query_grad_ref[...] = query_grad[...].astype(BF16)


def own_kernel(slot_ref, back_ref, key_grad_ref, value_grad_ref):
    slots, tokens = back_ref.shape[0], slot_ref.shape[0]
    ids = lax.broadcasted_iota(jnp.int32, (tokens, slots), 1)
    hot = (ids == slot_ref[...]).astype(F32).astype(BF16)
    rows = jnp.dot(hot, back_ref[...], preferred_element_type=F32).astype(BF16)
    key_grad_ref[...] = rows[:, :HD]
    value_grad_ref[...] = rows[:, HD:]


def weight_kernel(layer_ref, value_grad_ref, out_ref):
    for t in range(value_grad_ref.shape[0]):
        total = jnp.dot(layer_ref[0], value_grad_ref[t, 0], preferred_element_type=F32)
        for x in range(1, layer_ref.shape[0]):
            total += jnp.dot(layer_ref[x], value_grad_ref[t, x], preferred_element_type=F32)
        out_ref[:, t * HD : (t + 1) * HD] = total.astype(BF16)


def exact_pick(left, right):
    return lax.dot_general(left.astype(BF16), right.astype(BF16), NT, preferred_element_type=F32).astype(jnp.int32)


def shards(query_rows, key_rows, value_rows, output_grad, layer_input, token_document, token_offset, document_server):
    dp_size = lax.axis_size("z") * lax.axis_size("x")
    z_size = lax.axis_size("z")
    tokens = query_rows.shape[0]
    runs = tokens // RUN
    slots = dp_size * RUN
    width = query_rows.shape[1]
    group = width // HD
    me = lax.axis_index(DP)

    run_doc = token_document[::RUN]
    run_place = token_offset[::RUN] // RUN
    doc_ids = jnp.arange(document_server.shape[0], dtype=jnp.int32)
    run_server = jnp.sum(jnp.where(run_doc[:, None] == doc_ids[None, :], document_server[None, :], 0), axis=1)
    slot = (run_server[:, None] * RUN + jnp.arange(RUN, dtype=jnp.int32)[None, :]).reshape(tokens)

    sent = pl.pallas_call(
        pack_kernel,
        out_shape=jax.ShapeDtypeStruct((slots, 2 * width + 2 * HD), BF16),
        in_specs=[whole()] * 5,
        out_specs=whole(),
        compiler_params=params(),
        name="pack",
    )(slot[None, :], query_rows, output_grad, key_rows, value_rows)
    arrived = lax.all_to_all(
        sent.reshape(dp_size, RUN, -1), DP, split_axis=0, concat_axis=0, tiled=True
    ).reshape(slots, -1)

    tags = jnp.concatenate([run_doc, run_place, run_server])
    tags = jnp.pad(tags, (0, -tags.shape[0] % 128))
    all_tags = lax.all_gather(tags[None, :], DP, axis=0, tiled=True)
    all_doc, all_place, all_server = (all_tags[:, i * runs : (i + 1) * runs] for i in range(3))

    mine = all_server == me
    slot_doc = jnp.sum(jnp.where(mine, all_doc + 1, 0), axis=1) - 1
    slot_place = jnp.sum(jnp.where(mine, all_place, 0), axis=1)
    slot_doc = jnp.repeat(slot_doc, RUN)
    slot_pos = (slot_place[:, None] * RUN + jnp.arange(RUN, dtype=jnp.int32)[None, :]).reshape(slots)

    column = lambda at: pl.BlockSpec((slots, HD), lambda h, at=at: (0, at + h))
    fixed = lambda at: pl.BlockSpec((slots, HD), lambda h, at=at: (0, at))
    small = lambda shape: pl.BlockSpec(shape, lambda h: (0, 0))
    served = pl.pallas_call(
        functools.partial(server_kernel, group),
        grid=(group,),
        out_shape=jax.ShapeDtypeStruct((slots, 2 * HD), BF16),
        in_specs=[
            small((slots, 1)), small((slots, 1)), small((1, slots)), small((1, slots)),
            column(0), column(group), fixed(2 * group), fixed(2 * group + 1),
        ],
        out_specs=small((slots, 2 * HD)),
        scratch_shapes=[pltpu.VMEM((slots, slots), F32), pltpu.VMEM((slots, HD), F32), pltpu.VMEM((slots, HD), F32)],
        compiler_params=params(),
        name="server",
    )(slot_doc[:, None], slot_pos[:, None], slot_doc[None, :], slot_pos[None, :], arrived, arrived, arrived, arrived)

    back = lax.all_to_all(
        served.reshape(dp_size, RUN, -1), DP, split_axis=0, concat_axis=0, tiled=True
    ).reshape(slots, -1)
    key_grad, value_grad = pl.pallas_call(
        own_kernel,
        out_shape=[jax.ShapeDtypeStruct((tokens, HD), BF16)] * 2,
        in_specs=[whole()] * 2,
        out_specs=[whole()] * 2,
        compiler_params=params(),
        name="own",
    )(slot[:, None], back)

    part = width // X_SIZE
    turned = pl.pallas_call(
        functools.partial(turn_kernel, part // z_size),
        out_shape=jax.ShapeDtypeStruct((X_SIZE, part, tokens), BF16),
        in_specs=[whole()],
        out_specs=whole(),
        compiler_params=params(),
        name="turn",
    )(layer_input)
    layer_part = lax.all_to_all(turned, "x", split_axis=0, concat_axis=0, tiled=True)
    near = lax.all_gather(value_grad, "x", axis=0, tiled=False)
    all_value_grads = lax.all_gather(near, "t", axis=0, tiled=False)
    plane = pl.pallas_call(
        weight_kernel,
        out_shape=jax.ShapeDtypeStruct((part, all_value_grads.shape[0] * HD), BF16),
        in_specs=[whole()] * 2,
        out_specs=whole(),
        compiler_params=params(),
        name="weight",
    )(layer_part, all_value_grads)
    planes = lax.all_to_all(
        plane.reshape(z_size, part // z_size, -1), "z", split_axis=0, concat_axis=0, tiled=True
    )
    weight_grad = jnp.sum(planes.astype(F32), axis=0) * (1.0 / math.sqrt(tokens * dp_size))

    pairs = jnp.concatenate([key_rows, value_rows], axis=1)
    pairs, all_doc, all_place = lax.optimization_barrier((pairs, all_doc, all_place))
    all_pairs = lax.all_gather(pairs, DP, axis=0, tiled=True)
    same = run_doc[:, None] == all_doc.reshape(1, -1)
    at = jnp.arange(MAX_RUNS, dtype=jnp.int32)[:, None] == all_place.reshape(1, -1)
    ids = jnp.arange(dp_size * runs, dtype=jnp.int32)[None, :]
    place = exact_pick(same, jnp.where(at, ids // runs, 0)) * runs + exact_pick(same, jnp.where(at, ids % runs, 0))
    unroll = 4
    wide = (tokens, width)
    attended, query_grad = pl.pallas_call(
        functools.partial(home_kernel, group, unroll),
        out_shape=[jax.ShapeDtypeStruct(wide, BF16)] * 2,
        in_specs=[whole(pltpu.SMEM), whole(pltpu.SMEM), whole(), whole(), whole()],
        out_specs=[whole()] * 2,
        scratch_shapes=[
            pltpu.VMEM(all_pairs.shape, F32),
            pltpu.VMEM((unroll, MAX_RUNS * RUN, 2 * HD), F32),
            pltpu.VMEM(wide, F32), pltpu.VMEM(wide, F32), pltpu.VMEM(wide, F32), pltpu.VMEM(wide, F32),
        ],
        compiler_params=params(),
        name="home",
    )(place, run_place, query_rows, output_grad, all_pairs)
    return (attended, query_grad, key_grad, value_grad, weight_grad)


def solution(mesh):
    fine = Mesh(mesh.devices.reshape(-1, X_SIZE, mesh.shape["tensor"]), ("z", "x", "t"))
    rows = P(DP, "t")
    return jax.shard_map(
        shards,
        mesh=fine,
        in_specs=(rows, rows, rows, rows, rows, P(DP), P(DP), P()),
        out_specs=(rows, rows, rows, rows, P(("t",) + DP, None)),
        check_vma=False,
    )
```

time: 1090 us -> 483 us (0.44)
  waiting for transfers between devices: 919 us -> 180 us
  blocking collectives: 13.1 us -> 195 us
  local copies, waits for them, and re-layouts: 52 us -> 8.56 us
  Pallas kernels: 0 us -> 41.7 us
  matrix products: 39.1 us -> 0.51 us
    unnamed x2, waiting for transfers between devices: 690 us -> 0.03 us
    all_to_all x3, waiting for transfers between devices: 229 us -> 49.5 us  [the longest x1 31 us: shards(): lax.all_to_all(plane.reshape(z_size, part // z_size, -1), 'z', split_axis...]
    all_gather x1 -> x2, blocking collectives: 13.1 us -> 184 us  [the longest x1 171 us: shards(): all_tags = lax.all_gather(tags[None, :], DP, axis=0, tiled=True)]
    all_gather x0 -> x2, waiting for transfers between devices: none -> 130 us  [the longest x1 120 us: shards(): all_pairs = lax.all_gather(pairs, DP, axis=0, tiled=True)]
    pallas_call x0 -> x6, Pallas kernels: none -> 41.7 us  [the longest x1 26.4 us: shards(): pl.pallas_call(functools.partial(home_kernel, group, unroll), out_shape=[...]
    dot_general x49 -> x2, matrix products: 39.1 us -> 0.51 us  [exact_pick(): lax.dot_general(left.astype(BF16), right.astype(BF16), NT, preferred_elem...]
    gather x4 -> x0, local copies, waits for them, and re-layouts: 13 us -> none  [the longest x1 3.62 us: shards(): jnp.take(token_document, source_token)]
    dynamic_slice x24 -> x0, local copies, waits for them, and re-layouts: 12.9 us -> none  [the longest x16 8.27 us: pick(): return lax.dynamic_slice_in_dim(block, index * HD, HD, 1)]
  transfers between devices with their start and end apart: 4 -> 5, of which waited for: 4 -> 4; matrix products, arithmetic and copies ran while one was open for 1% -> 1% of each run, Pallas kernels for 0% -> 1%
where the time goes in v1:
time: 483 us
  blocking collectives  195 us (40%)
  waiting for transfers between devices  180 us (37%)
  Pallas kernels  41.7 us (9%)
  starting transfers between devices  40.4 us (8%)
  between operations  14.2 us (3%)
  local copies, waits for them, and re-layouts  8.56 us (2%)
    all_gather x1, blocking collectives, shards(): all_tags = lax.all_gather(tags[None, :], DP, axis=0, tiled=True)  171 us
    all_gather x1, waiting for transfers between devices, shards(): all_pairs = lax.all_gather(pairs, DP, axis=0, tiled=True)  120 us
    all_to_all x1, waiting for transfers between devices, shards(): lax.all_to_all(plane.reshape(z_size, part // z_size, -1), 'z', split_axis...  31 us
    pallas_call x1, Pallas kernels, shards(): pl.pallas_call(functools.partial(home_kernel, group, unroll), out_shape=[...  26.4 us
    all_to_all x1, starting transfers between devices, shards(): lax.all_to_all(sent.reshape(dp_size, RUN, -1), DP, split_axis=0, concat_a...  18.7 us
    all_to_all x1, waiting for transfers between devices, shards(): lax.all_to_all(served.reshape(dp_size, RUN, -1), DP, split_axis=0, concat...  18.5 us
    all_gather x1, blocking collectives, shards(): near = lax.all_gather(value_grad, 'x', axis=0, tiled=False)  13.2 us
    all_to_all x1, starting transfers between devices, shards(): lax.all_to_all(plane.reshape(z_size, part // z_size, -1), 'z', split_axis...  12.3 us
  transfers between devices with their start and end apart: 5, of which 4 were waited for; matrix products, arithmetic and copies ran while one was open for 1% of the time, Pallas kernels for 1%

profile of v1, /device:TPU:8, one launch (start us, length us, event | category | flops | bytes accessed | tf_op | source)
XLA Modules:
  0.0 482.6 jit_solution(971015609582154389)
XLA Ops:
  7.2 0.8 slice.15
  8.0 0.9 select_reduce_fusion.2
  9.0 1.0 copy-done.2
  10.0 1.0 copy-done.4
  11.1 0.8 copy-done.7
  11.9 0.8 copy-done.9
  12.8 0.8 pack.1
  13.6 1.4 copy-done
  15.1 18.7 %all-to-all-start = ((bf16[64,8,2304]{2,1,0:T(8,128)(2,1)}), bf16[64,8,2304]{2,1,0:T(8,128)(2,1)S(1)}, u32[]{:S(2)}, u32[]{:S(2)}) async-start(bf16[64,8,2304]{2,1,0:T(8,128)(2,1)} %bitcast.14), calls=%async_computation | async-start | bytes 4718592 | tf_op jit(solution)/shard_map/all_to_all | solution.py:186
  34.0 171.1 %all-gather.3 = s32[64,1,128]{2,1,0:T(1,128)S(1)} all-gather(s32[1,1,128]{2,1,0:T(1,128)S(1)} %pad_bitcast_fusion), channel_id=2, replica_groups=mesh['z'=16,'x'=4,'t'=8] {'z','x'}, dimensions={0}, use_global_device_ids=true | all-gather | bytes 33280 | tf_op jit(solution)/shard_map/all_gather | solution.py:192
  205.9 10.8 %server.1 = bf16[512,256]{1,0:T(8,128)(2,1)} custom-call(s32[512,1]{1,0:T(8,128)S(1)} %broadcast_in_dim_reshape.12.row_doc, s32[512,1]{1,0:T(8,128)S(1)} %add.115.row_pos, s32[1,512]{1,0:T(1,128)S(1)} %broadcast_in_dim_reshape.5.col_doc, s32[1,512]{1,0:T(1,128)S(1)} %add.112.col_pos, bf16[512,2304]{1,0:T(8,128)(2,1)S(1)} %bitcast.10, ...), custom_call_target="tpu_custom_call" | custom-call | tf_op jit(solution)/shard_map/server/pallas_call | solution.py:204
  216.8 9.3 %all-to-all-start.1 = ((bf16[64,8,256]{2,1,0:T(8,128)(2,1)}), bf16[64,8,256]{2,1,0:T(8,128)(2,1)S(1)}, u32[]{:S(2)}, u32[]{:S(2)}) async-start(bf16[64,8,256]{2,1,0:T(8,128)(2,1)} %bitcast.4), calls=%async_computation.1 | async-start | bytes 524288 | tf_op jit(solution)/shard_map/all_to_all | solution.py:218
  226.2 18.5 %all-to-all-done.1 = bf16[64,8,256]{2,1,0:T(8,128)(2,1)S(1)} async-done(((bf16[64,8,256]{2,1,0:T(8,128)(2,1)}), bf16[64,8,256]{2,1,0:T(8,128)(2,1)S(1)}, u32[]{:S(2)}, u32[]{:S(2)}) %all-to-all-start.1) | async-done | bytes 262176 | tf_op jit(solution)/shard_map/all_to_all | solution.py:218
  244.7 0.9 own.1
  245.6 13.2 %all-gather.1 = bf16[1024,128]{1,0:T(8,128)(2,1)} all-gather(bf16[256,128]{1,0:T(8,128)(2,1)} %get-tuple-element.10), channel_id=3, replica_groups=mesh['z'=16,'x'=4,'t'=8] {'x'}, dimensions={0}, use_global_device_ids=true | all-gather | bytes 327680 | tf_op jit(solution)/shard_map/all_gather | solution.py:240
  259.6 0.8 turn.1
  260.4 10.6 %all_to_all.20.layer_ref = bf16[4,256,256]{2,1,0:T(8,128)(2,1)S(1)} all-to-all(bf16[4,256,256]{2,1,0:T(8,128)(2,1)S(1)} %turn.1), channel_id=1, replica_groups=mesh['z'=16,'x'=4,'t'=8] {'x'}, dimensions={0} | all-to-all | bytes 1048576 | tf_op jit(solution)/shard_map/all_to_all | solution.py:239
  271.0 10.5 %all-gather.9.cloned.1.call-done = bf16[32,256,128]{2,1,0:T(8,128)(2,1)} async-done(((bf16[4,256,128]{2,1,0:T(8,128)(2,1)}), bf16[32,256,128]{2,1,0:T(8,128)(2,1)}) %all-gather.9.cloned.1.call-update) | async-done | bytes 2097168 | tf_op jit(solution)/shard_map/all_gather | solution.py:241
  281.5 1.6 copy-done.1
  283.1 2.0 weight.1
  285.1 12.3 %all-to-all-start.3 = ((bf16[16,16,1024]{2,1,0:T(8,128)(2,1)}), bf16[16,16,1024]{2,1,0:T(8,128)(2,1)S(1)}, u32[]{:S(2)}, u32[]{:S(2)}) async-start(bf16[16,16,1024]{2,1,0:T(8,128)(2,1)} %bitcast.8), calls=%async_computation.3 | async-start | bytes 1048576 | tf_op jit(solution)/shard_map/all_to_all | solution.py:250
  298.1 31.0 %all-to-all-done.3 = bf16[16,16,1024]{2,1,0:T(8,128)(2,1)S(1)} async-done(((bf16[16,16,1024]{2,1,0:T(8,128)(2,1)}), bf16[16,16,1024]{2,1,0:T(8,128)(2,1)S(1)}, u32[]{:S(2)}, u32[]{:S(2)}) %all-to-all-start.3) | async-done | bytes 524320 | tf_op jit(solution)/shard_map/all_to_all | solution.py:250
  329.9 119.6 %all-gather.7.cloned.1.call-done.pairs_ref = bf16[16384,256]{1,0:T(8,128)(2,1)} async-done(((bf16[256,256]{1,0:T(8,128)(2,1)}), bf16[16384,256]{1,0:T(8,128)(2,1)}) %all-gather.7.cloned.1.call-update) | async-done | bytes 8388624 | tf_op jit(solution)/shard_map/all_gather | solution.py:257
  449.4 26.4 %home.1 = (bf16[256,1024]{1,0:T(8,128)(2,1)}, bf16[256,1024]{1,0:T(8,128)(2,1)}) custom-call(s32[32,64]{1,0:T(8,128)S(1)} %fusion.place_ref, s32[32]{0:T(128)S(1)} %and_select_fusion.reach_ref, bf16[256,1024]{1,0:T(8,128)(2,1)S(1)} %copy-done.3, bf16[256,1024]{1,0:T(8,128)(2,1)S(1)} %copy-done.5, bf16[16384,256]{1,0:T(8,128)(2,1)} %all-gather.7.cloned.1.call-done.pairs_ref), custom_call_target="tpu_custom_call" | custom-call | tf_op jit(solution)/shard_map/home/pallas_call | solution.py:264
  (48 shorter events, 3.5 us)
Async XLA Ops:
  9.0 1.0 copy-start.2
  10.0 1.0 copy-start.4
  11.1 0.8 copy-start.7
  11.9 0.8 copy-start.9
  13.6 1.4 copy-start
  15.1 18.7 %copy-start.11 = (s32[256]{0:T(256)S(1)}, s32[256]{0:T(256)}, u32[]{:S(2)}) copy-start(s32[256]{0:T(256)} %param.14) | copy-start | bytes 3076
  15.1 190.8 %all-to-all-start = ((bf16[64,8,2304]{2,1,0:T(8,128)(2,1)}), bf16[64,8,2304]{2,1,0:T(8,128)(2,1)S(1)}, u32[]{:S(2)}, u32[]{:S(2)}) async-start(bf16[64,8,2304]{2,1,0:T(8,128)(2,1)} %bitcast.14), calls=%async_computation | async-start | bytes 4718592 | tf_op jit(solution)/shard_map/all_to_all | solution.py:186
  205.9 53.0 %copy-start.8 = (bf16[256,128]{1,0:T(8,128)(2,1)S(1)}, bf16[256,128]{1,0:T(8,128)(2,1)}, u32[]{:S(2)}) copy-start(bf16[256,128]{1,0:T(8,128)(2,1)} %key_ref.1) | copy-start | bytes 196612
  205.9 53.0 %copy-start.10 = (bf16[256,128]{1,0:T(8,128)(2,1)S(1)}, bf16[256,128]{1,0:T(8,128)(2,1)}, u32[]{:S(2)}) copy-start(bf16[256,128]{1,0:T(8,128)(2,1)} %value_ref.1) | copy-start | bytes 196612
  216.8 42.8 %copy-start.6 = (bf16[256,1024]{1,0:T(8,128)(2,1)S(1)}, bf16[256,1024]{1,0:T(8,128)(2,1)}, u32[]{:S(2)}) copy-start(bf16[256,1024]{1,0:T(8,128)(2,1)} %layer_ref.1) | copy-start | bytes 1572868
  216.8 27.9 %all-to-all-start.1 = ((bf16[64,8,256]{2,1,0:T(8,128)(2,1)}), bf16[64,8,256]{2,1,0:T(8,128)(2,1)S(1)}, u32[]{:S(2)}, u32[]{:S(2)}) async-start(bf16[64,8,256]{2,1,0:T(8,128)(2,1)} %bitcast.4), calls=%async_computation.1 | async-start | bytes 524288 | tf_op jit(solution)/shard_map/all_to_all | solution.py:218
  226.1 55.4 %all-gather.9.cloned.1.call-start = ((), (), s32[]{:S(2)}) async-start(), calls=%async_computation.5 | async-start | bytes 2359296 | tf_op jit(solution)/shard_map/all_gather | solution.py:241
  258.8 190.6 %all-gather.7.cloned.1.call-start = ((), (), s32[]{:S(2)}) async-start(), calls=%async_computation.4 | async-start | bytes 8519680 | tf_op jit(solution)/shard_map/all_gather | solution.py:257
  281.5 1.6 copy-start.1
  283.1 166.4 %copy-start.3 = (bf16[256,1024]{1,0:T(8,128)(2,1)S(1)}, bf16[256,1024]{1,0:T(8,128)(2,1)}, u32[]{:S(2)}) copy-start(bf16[256,1024]{1,0:T(8,128)(2,1)} %query_ref.3) | copy-start | bytes 1572868
  283.1 166.4 %copy-start.5 = (bf16[256,1024]{1,0:T(8,128)(2,1)S(1)}, bf16[256,1024]{1,0:T(8,128)(2,1)}, u32[]{:S(2)}) copy-start(bf16[256,1024]{1,0:T(8,128)(2,1)} %grad_ref.3) | copy-start | bytes 1572868
  285.1 44.0 %all-to-all-start.3 = ((bf16[16,16,1024]{2,1,0:T(8,128)(2,1)}), bf16[16,16,1024]{2,1,0:T(8,128)(2,1)S(1)}, u32[]{:S(2)}, u32[]{:S(2)}) async-start(bf16[16,16,1024]{2,1,0:T(8,128)(2,1)} %bitcast.8), calls=%async_computation.3 | async-start | bytes 1048576 | tf_op jit(solution)/shard_map/all_to_all | solution.py:250
Sparse Core Ops, SparseCore 0:
  259.0 22.4 all-gather.8
  285.0 164.3 all-gather.6

commit v2 on v1

v2 whole, which is shorter than its diff:
```python
import functools
import math

import jax
import jax.numpy as jnp
from jax import lax
from jax.experimental import pallas as pl
from jax.experimental.pallas import tpu as pltpu
from jax.sharding import Mesh
from jax.sharding import PartitionSpec as P

HD = 128
RUN = 8
X_SIZE = 4
Z_LOW = 4
MAX_RUNS = 64
STEP_RUNS = 16
BRING = 4
TAG_ROWS = 16
NEG_FILL = -1e30
F32 = jnp.float32
BF16 = jnp.bfloat16
NT = (((1,), (1,)), ((), ()))
TN = (((0,), (0,)), ((), ()))
DP = ("zh", "zl", "x")


def whole(memory=pltpu.VMEM):
    return pl.BlockSpec(memory_space=memory)


def params(limit):
    return pltpu.CompilerParams(vmem_limit_bytes=limit * 1024 * 1024)


def slot_row(doc, servers):
    tokens, docs = doc.shape[1], servers.shape[1]
    same = lax.broadcasted_iota(jnp.int32, (docs, tokens), 0) == doc
    names = jnp.broadcast_to(servers.astype(F32), (RUN, docs)).astype(BF16)
    server = jnp.dot(names, same.astype(F32).astype(BF16), preferred_element_type=F32)[:1].astype(jnp.int32)
    return server * RUN + lax.broadcasted_iota(jnp.int32, (1, tokens), 1) % RUN


def one_hot(slots, slot):
    return (lax.broadcasted_iota(jnp.int32, (slots, slot.shape[1]), 0) == slot).astype(F32).astype(BF16)


def pack_kernel(
    doc_hbm, offset_hbm, servers_hbm, query_hbm, grad_hbm, key_hbm, value_hbm, out_hbm, pairs_ref, slot_ref,
    doc_ref, offset_ref, servers_ref, query_ref, grad_ref, key_ref, value_ref, out_ref, in_sems, out_sems,
):
    slots, tokens = out_ref.shape[0], doc_ref.shape[1]
    sources = (doc_hbm, offset_hbm, servers_hbm, query_hbm, grad_hbm, key_hbm, value_hbm)
    targets = (doc_ref, offset_ref, servers_ref, query_ref, grad_ref, key_ref, value_ref)
    arrivals = [pltpu.make_async_copy(a, b, in_sems.at[i]) for i, (a, b) in enumerate(zip(sources, targets))]
    for copy in arrivals:
        copy.start()
    for copy in arrivals[:3]:
        copy.wait()
    doc = doc_ref[...]
    slot = slot_row(doc, servers_ref[...])
    slot_ref[...] = jnp.broadcast_to(slot, slot_ref.shape)
    hot = one_hot(slots, slot)
    place = offset_ref[...] // RUN
    line = lax.broadcasted_iota(jnp.int32, (HD, tokens), 0)
    tags = jnp.where(line == 0, doc + 1, jnp.where(line == 1, place, 0)).astype(F32).astype(BF16)
    tags = lax.dot_general(hot, tags, NT, preferred_element_type=F32).astype(BF16)
    departures = []

    def send(begin, end):
        columns = pl.ds(begin, end - begin)
        copy = pltpu.make_async_copy(out_ref.at[:, columns], out_hbm.at[:, columns], out_sems.at[len(departures)])
        copy.start()
        departures.append(copy)

    at = 0
    for copy, ref in zip(arrivals[3:], targets[3:]):
        copy.wait()
        width = ref.shape[1]
        out_ref[:, at : at + width] = jnp.dot(hot, ref[...], preferred_element_type=F32).astype(BF16)
        at += width
        if width > HD:
            send(at - width, at)
    out_ref[:, at : at + HD] = tags
    send(at - 2 * HD, at + HD)
    pairs_ref[:tokens, :HD] = key_ref[...]
    pairs_ref[:tokens, HD:] = value_ref[...]
    line = lax.broadcasted_iota(jnp.int32, (TAG_ROWS, tokens), 0)
    tags = jnp.where(line == 0, doc, jnp.where(line == 1, place, 0)).astype(F32).astype(BF16)
    pairs_ref[tokens:, :] = jnp.zeros((TAG_ROWS, 2 * HD), BF16)
    pairs_ref[tokens:, :tokens] = tags
    for copy in departures:
        copy.wait()


def turn_kernel(z_high, z_low, me_ref, layer_hbm, *refs):
    outs, layer_ref, sem = refs[:X_SIZE], refs[X_SIZE], refs[X_SIZE + 1]
    copy = pltpu.make_async_copy(layer_hbm, layer_ref, sem)
    copy.start()
    width = layer_ref.shape[1]
    rows = width // X_SIZE
    deep = rows // (z_high * z_low)
    new = lax.broadcasted_iota(jnp.int32, (rows, width), 0)
    old = lax.broadcasted_iota(jnp.int32, (rows, width), 1)
    ahead = old - (new // deep * (X_SIZE * deep) + new % deep)
    copy.wait()
    for d in range(X_SIZE):
        hot = (ahead == (me_ref[0] + d) % X_SIZE * deep).astype(F32).astype(BF16)
        outs[d][...] = lax.dot_general(hot, layer_ref[...], NT, preferred_element_type=F32).astype(BF16)


def server_kernel(group, tag_ref, query_ref, grad_ref, key_ref, value_ref, out_ref, bias, key_acc, value_acc):
    head = pl.program_id(0)

    @pl.when(head == 0)
    def _():
        slots = tag_ref.shape[0]
        tags = tag_ref[...].astype(F32)
        turned = tags.T
        col_doc, row_doc = tags[:, 0:1], turned[0:1, :]
        col_pos = tags[:, 1:2] * RUN + (lax.broadcasted_iota(jnp.int32, (slots, 1), 0) % RUN).astype(F32)
        row_pos = turned[1:2, :] * RUN + (lax.broadcasted_iota(jnp.int32, (1, slots), 1) % RUN).astype(F32)
        bias[...] = jnp.where((col_doc == row_doc) & (col_pos <= row_pos), 0.0, NEG_FILL)
        key_acc[...] = jnp.zeros_like(key_acc)
        value_acc[...] = jnp.zeros_like(value_acc)

    scale = float(HD) ** (-0.5)
    query, grad = query_ref[...], grad_ref[...]
    scores = lax.dot_general(key_ref[...], query, NT, preferred_element_type=F32) + bias[...]
    top = jnp.max(scores, axis=0, keepdims=True)
    exp_scores = jnp.exp((scores - top) * scale)
    total = jnp.sum(exp_scores, axis=0, keepdims=True)
    weights = exp_scores * (1.0 / total)
    weights_low = weights.astype(BF16)
    grad_weights = lax.dot_general(value_ref[...], grad, NT, preferred_element_type=F32)
    row_delta = jnp.sum(weights_low.astype(F32) * grad_weights, axis=0, keepdims=True)
    grad_scores = (weights * (grad_weights - row_delta)).astype(BF16)
    value_acc[...] += jnp.dot(weights_low, grad, preferred_element_type=F32)
    key_acc[...] += jnp.dot(grad_scores, query, preferred_element_type=F32)

    @pl.when(head == group - 1)
    def _():
        out_ref[:, :HD] = (key_acc[...] * scale).astype(BF16)
        out_ref[:, HD:] = value_acc[...].astype(BF16)


def home_kernel(
    group, unroll, place_ref, reach_ref, query_hbm, grad_hbm, pairs_ref, mixed_ref, query_grad_ref,
    rows, query_ref, grad_ref, query, grad, mixed, query_grad, sems,
):
    scale = float(HD) ** (-0.5)
    count = query_ref.shape[0] // RUN
    arrivals = [
        pltpu.make_async_copy(query_hbm, query_ref, sems.at[0]),
        pltpu.make_async_copy(grad_hbm, grad_ref, sems.at[1]),
    ]
    for copy in arrivals:
        copy.start()
    rows[...] = jnp.zeros_like(rows)
    for copy in arrivals:
        copy.wait()
    query[...] = query_ref[...].astype(F32)
    grad[...] = grad_ref[...].astype(F32)

    def stack(ref, run):
        parts = [ref[pl.ds(pl.multiple_of(run * RUN, RUN), RUN), h * HD : (h + 1) * HD] for h in range(group)]
        return jnp.concatenate(parts, axis=0)

    def unstack(ref, run, block):
        for h in range(group):
            ref[pl.ds(pl.multiple_of(run * RUN, RUN), RUN), h * HD : (h + 1) * HD] = block[h * RUN : (h + 1) * RUN]

    def bring(u, run):
        def several(i, carry):
            for j in range(BRING):
                k = i * BRING + j
                place = place_ref[run, k]
                two = pairs_ref[pl.ds(pl.multiple_of(place // 2 * (2 * RUN), 2 * RUN), 2 * RUN), :].astype(F32)
                one = jnp.where(place % 2 == 1, two[RUN:], two[:RUN])
                rows[u, pl.ds(pl.multiple_of(k * RUN, RUN), RUN), :] = one
            return carry

        lax.fori_loop(0, reach_ref[run] // BRING + 1, several, 0)

    def part(index, reach_runs):
        reach_rows = reach_runs * RUN
        for u in range(unroll):
            bring(u, index * unroll + u)
        rows_each = group * RUN
        token = lax.broadcasted_iota(jnp.int32, (rows_each, reach_rows), 0) % RUN
        ahead = lax.broadcasted_iota(jnp.int32, (rows_each, reach_rows), 1) - token
        each = range(unroll)
        cut = lambda block: [block[u * rows_each : (u + 1) * rows_each] for u in each]
        runs = [index * unroll + u for u in each]
        blocks = [rows[u, :reach_rows].astype(BF16) for u in each]
        keys, values = [block[:, :HD] for block in blocks], [block[:, HD:] for block in blocks]
        query_runs = [stack(query, run).astype(BF16) for run in runs]
        grad_full = jnp.concatenate([stack(grad, run) for run in runs], axis=0)
        grad_runs = cut(grad_full.astype(BF16))
        dots = lambda left, right: [lax.dot_general(left[u], right[u], NT, preferred_element_type=F32) for u in each]
        scores = dots(query_runs, keys)
        scores = [jnp.where(ahead <= reach_ref[runs[u]] * RUN, scores[u], NEG_FILL) for u in each]
        scores = jnp.concatenate(scores, axis=0)
        grad_weights = jnp.concatenate(dots(grad_runs, values), axis=0)
        top = jnp.max(scores, axis=1, keepdims=True)
        exp_scores = jnp.exp((scores - top) * scale)
        total = jnp.sum(exp_scores, axis=1, keepdims=True)
        weights = exp_scores * (1.0 / total)
        low = cut(weights.astype(BF16))
        mixed_full = [jnp.dot(low[u], values[u], preferred_element_type=F32) for u in each]
        row_delta = jnp.sum(grad_full * jnp.concatenate(mixed_full, axis=0), axis=1, keepdims=True)
        grad_scores = cut((weights * (grad_weights - row_delta)).astype(BF16))
        back = [jnp.dot(grad_scores[u], keys[u], preferred_element_type=F32) * scale for u in each]
        for u in each:
            unstack(mixed, runs[u], mixed_full[u])
            unstack(query_grad, runs[u], back[u])

    def step(index, carry):
        reach = reach_ref[index * unroll]
        for u in range(1, unroll):
            reach = jnp.maximum(reach, reach_ref[index * unroll + u])
        below = 0
        for reach_runs in (STEP_RUNS, 2 * STEP_RUNS, MAX_RUNS):
            pl.when((reach >= below) & (reach < reach_runs))(functools.partial(part, index, reach_runs))
            below = reach_runs
        return carry

    lax.fori_loop(0, count // unroll, step, 0)
    mixed_ref[...] = mixed[...].astype(BF16)
    query_grad_ref[...] = query_grad[...].astype(BF16)


def own_kernel(slot_ref, back_ref, key_grad_ref, value_grad_ref, near_ref):
    hot = one_hot(back_ref.shape[0], slot_ref[:1])
    rows = lax.dot_general(hot, back_ref[...], TN, preferred_element_type=F32).astype(BF16)
    key_grad_ref[...] = rows[:, :HD]
    value_grad_ref[...] = rows[:, HD:]
    for i in range(near_ref.shape[0]):
        near_ref[i] = rows[:, HD:]


def weight_kernel(x_ref, core_ref, *refs):
    layers, own_ref, other_ref, out_ref = refs[:X_SIZE], refs[X_SIZE], refs[X_SIZE + 1], refs[X_SIZE + 2]
    me, core = x_ref[0], core_ref[0]
    y_size = own_ref.shape[0] // X_SIZE
    for y in range(y_size):
        for grads, c in ((own_ref, core), (other_ref, 1 - core)):
            total = jnp.dot(layers[0][...], grads[me * y_size + y], preferred_element_type=F32)
            for d in range(1, X_SIZE):
                there = (me - d + X_SIZE) % X_SIZE
                total += jnp.dot(layers[d][...], grads[there * y_size + y], preferred_element_type=F32)
            out_ref[:, pl.ds(pl.multiple_of((2 * y + c) * HD, HD), HD)] = total.astype(BF16)


def exact_pick(left, right):
    return lax.dot_general(left.astype(BF16), right.astype(BF16), NT, preferred_element_type=F32).astype(jnp.int32)


def shards(query_rows, key_rows, value_rows, output_grad, layer_input, token_document, token_offset, document_server):
    dp_size = lax.axis_size(DP)
    high, low = lax.axis_size("zh"), lax.axis_size("zl")
    tokens = query_rows.shape[0]
    runs = tokens // RUN
    slots = dp_size * RUN
    width = query_rows.shape[1]
    group = width // HD
    doc, offset, servers = token_document[None, :], token_offset[None, :], document_server[None, :]
    x_index, core = lax.axis_index("x").astype(jnp.int32), lax.axis_index("c").astype(jnp.int32)
    x_index, core = x_index.reshape(1), core.reshape(1)

    def call(kernel, out_shape, *args, **more):
        shapes = [jax.ShapeDtypeStruct(shape, BF16) if isinstance(shape, tuple) else shape for shape in out_shape]
        out = pl.pallas_call(
            kernel,
            out_shape=shapes,
            in_specs=more.pop("in_specs", [whole()] * len(args)),
            out_specs=more.pop("out_specs", [whole()] * len(shapes)),
            compiler_params=params(more.pop("limit", 32)),
            **more,
        )(*args)
        return out[0] if len(shapes) == 1 else list(out)

    def swap(block, axis):
        return lax.all_to_all(block, axis, split_axis=0, concat_axis=0, tiled=True)

    sent, pairs, slot = call(
        pack_kernel,
        [(slots, 2 * width + 3 * HD), (tokens + TAG_ROWS, 2 * HD), jax.ShapeDtypeStruct((RUN, tokens), jnp.int32)],
        doc, offset, servers, query_rows, output_grad, key_rows, value_rows,
        in_specs=[whole(pltpu.HBM)] * 7,
        out_specs=[whole(pltpu.HBM), whole(), whole()],
        scratch_shapes=[pltpu.VMEM((1, tokens), jnp.int32)] * 2 + [pltpu.VMEM(servers.shape, jnp.int32)]
        + [pltpu.VMEM((tokens, width), BF16)] * 2 + [pltpu.VMEM((tokens, HD), BF16)] * 2
        + [pltpu.VMEM((slots, 2 * width + 3 * HD), BF16), pltpu.SemaphoreType.DMA((7,)), pltpu.SemaphoreType.DMA((3,))],
        limit=60,
        name="pack",
    )
    part = width // X_SIZE
    sent, layer_input, pairs = lax.optimization_barrier((sent, layer_input, pairs))
    arrived = swap(sent.reshape(dp_size, RUN, -1), DP)
    turned = call(
        functools.partial(turn_kernel, high, low), [(part, tokens)] * X_SIZE, x_index, layer_input,
        in_specs=[whole(pltpu.SMEM), whole(pltpu.HBM)],
        scratch_shapes=[pltpu.VMEM((tokens, width), BF16), pltpu.SemaphoreType.DMA],
        limit=60,
        name="turn",
    )
    turned[0], pairs = lax.optimization_barrier((turned[0], pairs))
    all_pairs = lax.all_gather(pairs, DP, axis=0, tiled=True)
    layers = [turned[0]] + [
        lax.ppermute(turned[d], "x", [(i, (i + d) % X_SIZE) for i in range(X_SIZE)]) for d in range(1, X_SIZE)
    ]
    arrived, *layers = lax.optimization_barrier((arrived, *layers))
    arrived = arrived.reshape(slots, -1)

    column = lambda at: pl.BlockSpec((slots, HD), lambda h, at=at: (0, at + h))
    fixed = lambda at: pl.BlockSpec((slots, HD), lambda h, at=at: (0, at))
    served = call(
        functools.partial(server_kernel, group), [(slots, 2 * HD)], *[arrived] * 5,
        grid=(group,),
        in_specs=[fixed(2 * group + 2), column(0), column(group), fixed(2 * group), fixed(2 * group + 1)],
        out_specs=[pl.BlockSpec((slots, 2 * HD), lambda h: (0, 0))],
        scratch_shapes=[pltpu.VMEM((slots, slots), F32), pltpu.VMEM((slots, HD), F32), pltpu.VMEM((slots, HD), F32)],
        name="server",
    )

    back = swap(served.reshape(dp_size, RUN, -1), DP).reshape(slots, -1)
    key_grad, value_grad, near = call(
        own_kernel, [(tokens, HD), (tokens, HD), (X_SIZE * lax.axis_size("y"), tokens, HD)], slot, back, name="own"
    )

    y_size = lax.axis_size("y")
    own_core = swap(near, ("x", "y"))
    other_core = lax.ppermute(own_core, "c", [(0, 1), (1, 0)])
    channels = 2 * y_size * HD
    plane = call(
        weight_kernel, [(part, channels)], x_index, core, *layers, own_core, other_core,
        in_specs=[whole(pltpu.SMEM)] * 2 + [whole()] * (X_SIZE + 2), name="weight",
    )
    plane, all_pairs = lax.optimization_barrier((plane, all_pairs))
    block = swap(plane.reshape(high * low, part // (high * low), channels), ("zh", "zl"))
    weight_grad = jnp.sum(block.astype(F32), axis=0) * (1.0 / math.sqrt(tokens * dp_size))

    tags = all_pairs.reshape(dp_size, tokens + TAG_ROWS, 2 * HD)[:, tokens : tokens + 2, :tokens:RUN]
    all_doc, all_place = tags[:, 0].reshape(1, -1), tags[:, 1].reshape(1, -1)
    run_doc, run_place = token_document[::RUN], token_offset[::RUN] // RUN
    same = run_doc.astype(BF16)[:, None] == all_doc
    at = jnp.arange(MAX_RUNS, dtype=jnp.int32).astype(BF16)[:, None] == all_place
    ids = jnp.arange(dp_size * runs, dtype=jnp.int32)[None, :]
    device, run = exact_pick(same, jnp.where(at, ids // runs, 0)), exact_pick(same, jnp.where(at, ids % runs, 0))
    place = device * (runs + TAG_ROWS // RUN) + run
    unroll = 8
    wide = (tokens, width)
    attended, query_grad = call(
        functools.partial(home_kernel, group, unroll), [wide, wide],
        place, run_place, query_rows, output_grad, all_pairs,
        in_specs=[whole(pltpu.SMEM), whole(pltpu.SMEM), whole(pltpu.HBM), whole(pltpu.HBM), whole()],
        scratch_shapes=[pltpu.VMEM((unroll, MAX_RUNS * RUN, 2 * HD), F32)] + [pltpu.VMEM(wide, BF16)] * 2
        + [pltpu.VMEM(wide, F32)] * 4 + [pltpu.SemaphoreType.DMA((2,))],
        limit=60,
        name="home",
    )
    return (attended, query_grad, key_grad, value_grad, weight_grad)


def solution(mesh):
    shape = (-1, Z_LOW, X_SIZE, mesh.shape["tensor"] // 2, 2)
    fine = Mesh(mesh.devices.reshape(shape), ("zh", "zl", "x", "y", "c"))
    rows = P(DP, ("y", "c"))
    return jax.shard_map(
        shards,
        mesh=fine,
        in_specs=(rows, rows, rows, rows, rows, P(DP), P(DP), P()),
        out_specs=(rows, rows, rows, rows, P(("y", "c") + DP, None)),
        check_vma=False,
    )
```

time: 483 us -> 275 us (0.57)
  the two profiles are of different devices: /device:TPU:8 before, /device:TPU:32 now
where the time goes in v2:
time: 275 us; the launch traced here: 274 us
  waiting for transfers between devices  134 us (49%)
  blocking collectives  49.6 us (18%)
  starting transfers between devices  37.7 us (14%)
  Pallas kernels  32.9 us (12%)
  between operations  14.2 us (5%)
  local copies, waits for them, and re-layouts  3.04 us (1%)
    all_to_all x2, waiting for transfers between devices, swap(): return lax.all_to_all(block, axis, split_axis=0, concat_axis=0, tiled=True)  128 us
    all_to_all x2, blocking collectives, swap(): return lax.all_to_all(block, axis, split_axis=0, concat_axis=0, tiled=True)  49.6 us
    pallas_call x6, Pallas kernels, call(): pl.pallas_call(kernel, out_shape=shapes, in_specs=more.pop('in_specs', [w...  32.9 us
    all_to_all x2, starting transfers between devices, swap(): return lax.all_to_all(block, axis, split_axis=0, concat_axis=0, tiled=True)  24.3 us
    ppermute x3, starting transfers between devices, shards(): lax.ppermute(turned[d], 'x', [(i, (i + d) % X_SIZE) for i in range(X_SIZE)])  11.3 us
  transfers between devices with their start and end apart: 7, of which 5 were waited for; matrix products, arithmetic and copies ran while one was open for 2% of the time, Pallas kernels for 10%

profile of v2, /device:TPU:32, one launch (start us, length us, event | category | flops | bytes accessed | tf_op | source)
XLA Modules:
  0.0 274.1 jit_solution(9616950591185871203)
XLA Ops:
  7.2 4.1 %pack.1 = (bf16[512,2432]{1,0:T(8,128)(2,1)}, bf16[272,256]{1,0:T(8,128)(2,1)}, s32[8,256]{1,0:T(8,128)}) custom-call(s32[1,256]{1,0:T(1,128)} %bitcast.21, s32[1,256]{1,0:T(1,128)} %bitcast.22, s32[1,256]{1,0:T(1,128)} %bitcast.20, bf16[256,1024]{1,0:T(8,128)(2,1)} %query_hbm.3, bf16[256,1024]{1,0:T(8,128)(2,1)} %grad_hbm.3, bf16[256,128]{1,0:T(8,128)(2,1)} %key_hbm.1, ...), custom_call_target="tpu_custom_call" | custom-call | tf_op jit(solution)/shard_map/pack/pallas_call | solution.py:273
  11.3 2.5 turn.1
  13.9 18.4 %all-to-all-start = ((bf16[64,8,2432]{2,1,0:T(8,128)(2,1)}), bf16[64,8,2432]{2,1,0:T(8,128)(2,1)S(1)}, u32[]{:S(2)}, u32[]{:S(2)}) async-start(bf16[64,8,2432]{2,1,0:T(8,128)(2,1)} %bitcast.19), calls=%async_computation | async-start | bytes 4980736 | tf_op jit(solution)/shard_map/all_to_all | solution.py:284
  32.3 3.4 %collective-permute-start = (bf16[256,256]{1,0:T(8,128)(2,1)S(1)}, bf16[256,256]{1,0:T(8,128)(2,1)S(1)}, u32[]{:S(2)}, u32[]{:S(2)}) collective-permute-start(bf16[256,256]{1,0:T(8,128)(2,1)S(1)} %copy-done.6), channel_id=1, source_target_pairs={{0,8},{8,16},{16,24},{24,0},{1,9},{9,17},{17,25},{25,1},{2,10},{10... | collective-permute-start | bytes 393224 | tf_op jit(solution)/shard_map/ppermute | solution.py:311
  35.6 4.6 %collective-permute-start.1 = (bf16[256,256]{1,0:T(8,128)(2,1)S(1)}, bf16[256,256]{1,0:T(8,128)(2,1)S(1)}, u32[]{:S(2)}, u32[]{:S(2)}) collective-permute-start(bf16[256,256]{1,0:T(8,128)(2,1)S(1)} %copy-done.5), channel_id=1, source_target_pairs={{0,16},{8,24},{16,0},{24,8},{1,17},{9,25},{17,1},{25,9},{2,18},{10... | collective-permute-start | bytes 393224 | tf_op jit(solution)/shard_map/ppermute | solution.py:311
  40.2 3.4 %collective-permute-start.2 = (bf16[256,256]{1,0:T(8,128)(2,1)S(1)}, bf16[256,256]{1,0:T(8,128)(2,1)S(1)}, u32[]{:S(2)}, u32[]{:S(2)}) collective-permute-start(bf16[256,256]{1,0:T(8,128)(2,1)S(1)} %copy-done.4), channel_id=1, source_target_pairs={{0,24},{8,0},{16,8},{24,16},{1,25},{9,1},{17,9},{25,17},{2,26},{10... | collective-permute-start | bytes 393224 | tf_op jit(solution)/shard_map/ppermute | solution.py:311
  43.6 3.8 %collective-permute-done.1.refs_2_ = bf16[256,256]{1,0:T(8,128)(2,1)S(1)} collective-permute-done((bf16[256,256]{1,0:T(8,128)(2,1)S(1)}, bf16[256,256]{1,0:T(8,128)(2,1)S(1)}, u32[]{:S(2)}, u32[]{:S(2)}) %collective-permute-start.1) | collective-permute-done | bytes 131104 | tf_op jit(solution)/shard_map/ppermute | solution.py:311
  47.5 115.4 %all-to-all-done = bf16[64,8,2432]{2,1,0:T(8,128)(2,1)S(1)} async-done(((bf16[64,8,2432]{2,1,0:T(8,128)(2,1)}), bf16[64,8,2432]{2,1,0:T(8,128)(2,1)S(1)}, u32[]{:S(2)}, u32[]{:S(2)}) %all-to-all-start) | async-done | bytes 2490400 | tf_op jit(solution)/shard_map/all_to_all | solution.py:284
  163.0 10.2 %server.1 = bf16[512,256]{1,0:T(8,128)(2,1)S(1)} custom-call(bf16[512,2432]{1,0:T(8,128)(2,1)S(1)} %bitcast.11, bf16[512,2432]{1,0:T(8,128)(2,1)S(1)} %bitcast.12, bf16[512,2432]{1,0:T(8,128)(2,1)S(1)} %bitcast.13, bf16[512,2432]{1,0:T(8,128)(2,1)S(1)} %bitcast.14, bf16[512,2432]{1,0:T(8,128)(2,1)S(1)} %bitcast.15), custom_call_target="tpu_custom_call" | custom-call | tf_op jit(solution)/shard_map/server/pallas_call | solution.py:273
  173.2 29.9 %all_to_all.20 = bf16[64,8,256]{2,1,0:T(8,128)(2,1)S(1)} all-to-all(bf16[64,8,256]{2,1,0:T(8,128)(2,1)S(1)} %bitcast.16), channel_id=1, replica_groups=mesh['zh'=4,'zl'=4,'x'=4,'y'=4,'c'=2] {'zh','zl','x'}, dimensions={0} | all-to-all | bytes 524288 | tf_op jit(solution)/shard_map/all_to_all | solution.py:284
  203.1 1.0 own.1
  204.0 19.7 %all_to_all.21.refs_4_ = bf16[16,256,128]{2,1,0:T(8,128)(2,1)S(1)} all-to-all(bf16[16,256,128]{2,1,0:T(8,128)(2,1)S(1)} %get-tuple-element.45), channel_id=1, replica_groups=mesh['zh'=4,'zl'=4,'x'=4,'y'=4,'c'=2] {'x','y'}, dimensions={0} | all-to-all | bytes 2097152 | tf_op jit(solution)/shard_map/all_to_all | solution.py:284
  223.8 2.0 collective-permute-start.3
  225.8 2.6 collective-permute-done.3.refs_5_
  228.4 2.1 weight.1
  230.5 5.9 %all-to-all-start.3 = ((bf16[16,16,1024]{2,1,0:T(8,128)(2,1)}), bf16[16,16,1024]{2,1,0:T(8,128)(2,1)S(1)}, u32[]{:S(2)}, u32[]{:S(2)}) async-start(bf16[16,16,1024]{2,1,0:T(8,128)(2,1)} %bitcast.10), calls=%async_computation.3 | async-start | bytes 1048576 | tf_op jit(solution)/shard_map/all_to_all | solution.py:284
  236.8 0.5 and_select_fusion.reach_ref
  237.3 2.4 slice.17
  239.7 0.2 slice_reduce_fusion.1
  240.1 0.3 fusion.1
  240.4 0.9 fusion.place_ref
  241.2 13.0 %home.1 = (bf16[256,1024]{1,0:T(8,128)(2,1)}, bf16[256,1024]{1,0:T(8,128)(2,1)}) custom-call(s32[32,64]{1,0:T(8,128)} %fusion.place_ref, s32[32]{0:T(128)} %and_select_fusion.reach_ref, bf16[256,1024]{1,0:T(8,128)(2,1)} %query_hbm.3, bf16[256,1024]{1,0:T(8,128)(2,1)} %grad_hbm.3, bf16[17408,256]{1,0:T(8,128)(2,1)} %all-gather.2.cloned.1.call-done.pairs_ref), custom_call_target="tpu_custom_call" | custom-call | tf_op jit(solution)/shard_map/home/pallas_call | solution.py:273
  254.3 12.3 %all-to-all-done.3 = bf16[16,16,1024]{2,1,0:T(8,128)(2,1)S(1)} async-done(((bf16[16,16,1024]{2,1,0:T(8,128)(2,1)}), bf16[16,16,1024]{2,1,0:T(8,128)(2,1)S(1)}, u32[]{:S(2)}, u32[]{:S(2)}) %all-to-all-start.3) | async-done | bytes 524320 | tf_op jit(solution)/shard_map/all_to_all | solution.py:284
  266.6 0.6 broadcast_multiply_fusion
  (28 shorter events, 0.7 us)
Async XLA Ops:
  7.2 223.3 %all-gather.2.cloned.1.call-start = ((), (), s32[]{:S(2)}) async-start(), calls=%async_computation.4 | async-start | bytes 9052160 | tf_op jit(solution)/shard_map/all_gather | solution.py:309
  13.8 18.4 %copy-start.6 = (bf16[256,256]{1,0:T(8,128)(2,1)S(1)}, bf16[256,256]{1,0:T(8,128)(2,1)}, u32[]{:S(2)}) copy-start(bf16[256,256]{1,0:T(8,128)(2,1)} %get-tuple-element.36) | copy-start | bytes 393220
  13.9 21.8 %copy-start.5 = (bf16[256,256]{1,0:T(8,128)(2,1)S(1)}, bf16[256,256]{1,0:T(8,128)(2,1)}, u32[]{:S(2)}) copy-start(bf16[256,256]{1,0:T(8,128)(2,1)} %get-tuple-element.37) | copy-start | bytes 393220
  13.9 26.4 %copy-start.4 = (bf16[256,256]{1,0:T(8,128)(2,1)S(1)}, bf16[256,256]{1,0:T(8,128)(2,1)}, u32[]{:S(2)}) copy-start(bf16[256,256]{1,0:T(8,128)(2,1)} %get-tuple-element.38) | copy-start | bytes 393220
  13.9 149.1 %all-to-all-start = ((bf16[64,8,2432]{2,1,0:T(8,128)(2,1)}), bf16[64,8,2432]{2,1,0:T(8,128)(2,1)S(1)}, u32[]{:S(2)}, u32[]{:S(2)}) async-start(bf16[64,8,2432]{2,1,0:T(8,128)(2,1)} %bitcast.19), calls=%async_computation | async-start | bytes 4980736 | tf_op jit(solution)/shard_map/all_to_all | solution.py:284
  32.3 11.4 %collective-permute-start = (bf16[256,256]{1,0:T(8,128)(2,1)S(1)}, bf16[256,256]{1,0:T(8,128)(2,1)S(1)}, u32[]{:S(2)}, u32[]{:S(2)}) collective-permute-start(bf16[256,256]{1,0:T(8,128)(2,1)S(1)} %copy-done.6), channel_id=1, source_target_pairs={{0,8},{8,16},{16,24},{24,0},{1,9},{9,17},{17,25},{25,1},{2,10},{10... | collective-permute-start | bytes 393224 | tf_op jit(solution)/shard_map/ppermute | solution.py:311
  35.6 11.8 %collective-permute-start.1 = (bf16[256,256]{1,0:T(8,128)(2,1)S(1)}, bf16[256,256]{1,0:T(8,128)(2,1)S(1)}, u32[]{:S(2)}, u32[]{:S(2)}) collective-permute-start(bf16[256,256]{1,0:T(8,128)(2,1)S(1)} %copy-done.5), channel_id=1, source_target_pairs={{0,16},{8,24},{16,0},{24,8},{1,17},{9,25},{17,1},{25,9},{2,18},{10... | collective-permute-start | bytes 393224 | tf_op jit(solution)/shard_map/ppermute | solution.py:311
  40.2 7.3 %collective-permute-start.2 = (bf16[256,256]{1,0:T(8,128)(2,1)S(1)}, bf16[256,256]{1,0:T(8,128)(2,1)S(1)}, u32[]{:S(2)}, u32[]{:S(2)}) collective-permute-start(bf16[256,256]{1,0:T(8,128)(2,1)S(1)} %copy-done.4), channel_id=1, source_target_pairs={{0,24},{8,0},{16,8},{24,16},{1,25},{9,1},{17,9},{25,17},{2,26},{10... | collective-permute-start | bytes 393224 | tf_op jit(solution)/shard_map/ppermute | solution.py:311
  163.0 40.1 %copy-start.1 = (s32[8,256]{1,0:T(8,128)S(1)}, s32[8,256]{1,0:T(8,128)}, u32[]{:S(2)}) copy-start(s32[8,256]{1,0:T(8,128)} %get-tuple-element.43.slot_ref) | copy-start | bytes 24580
  173.2 55.2 %copy-start = (bf16[256,256]{1,0:T(8,128)(2,1)S(1)}, bf16[256,256]{1,0:T(8,128)(2,1)}, u32[]{:S(2)}) copy-start(bf16[256,256]{1,0:T(8,128)(2,1)} %get-tuple-element.39.refs_0_) | copy-start | bytes 393220
  223.8 12.7 %copy-start.2 = (s32[256]{0:T(256)S(1)}, s32[256]{0:T(256)}, u32[]{:S(2)}) copy-start(s32[256]{0:T(256)} %param.13) | copy-start | bytes 3076
  223.8 12.7 %copy-start.3 = (s32[256]{0:T(256)S(1)}, s32[256]{0:T(256)}, u32[]{:S(2)}) copy-start(s32[256]{0:T(256)} %param.14) | copy-start | bytes 3076
  223.8 4.7 %collective-permute-start.3 = (bf16[16,256,128]{2,1,0:T(8,128)(2,1)S(1)}, bf16[16,256,128]{2,1,0:T(8,128)(2,1)S(1)}, u32[]{:S(2)}, u32[]{:S(2)}) collective-permute-start(bf16[16,256,128]{2,1,0:T(8,128)(2,1)S(1)} %all_to_all.21.refs_4_), channel_id=1, source_target_pairs={{0,1},{1,0},{2,3},{3,2},{4,5},{5,4},{6,7},{7,6},{8,9},{9,8},{10,11... | collective-permute-start | bytes 3145736 | tf_op jit(solution)/shard_map/ppermute | solution.py:334
  230.5 36.0 %all-to-all-start.3 = ((bf16[16,16,1024]{2,1,0:T(8,128)(2,1)}), bf16[16,16,1024]{2,1,0:T(8,128)(2,1)S(1)}, u32[]{:S(2)}, u32[]{:S(2)}) async-start(bf16[16,16,1024]{2,1,0:T(8,128)(2,1)} %bitcast.10), calls=%async_computation.3 | async-start | bytes 1048576 | tf_op jit(solution)/shard_map/all_to_all | solution.py:284
Sparse Core Ops, SparseCore 0:
  14.0 208.2 all-gather.1

commit v3 on v2

--- a/solution.py
+++ b/solution.py
@@ -16,6 +16,8 @@
 MAX_RUNS = 64
 STEP_RUNS = 16
 BRING = 4
+LOG2_E = math.log2(math.e)
+SERVER_HEADS = 4
 TAG_ROWS = 16
 NEG_FILL = -1e30
 F32 = jnp.float32
@@ -109,7 +111,7 @@
         outs[d][...] = lax.dot_general(hot, layer_ref[...], NT, preferred_element_type=F32).astype(BF16)
 
 
-def server_kernel(group, tag_ref, query_ref, grad_ref, key_ref, value_ref, out_ref, bias, key_acc, value_acc):
+def server_kernel(tag_ref, query_ref, grad_ref, key_ref, value_ref, out_ref, bias, key_acc, value_acc):
     head = pl.program_id(0)
 
     @pl.when(head == 0)
@@ -125,20 +127,27 @@
         value_acc[...] = jnp.zeros_like(value_acc)
 
     scale = float(HD) ** (-0.5)
-    query, grad = query_ref[...], grad_ref[...]
-    scores = lax.dot_general(key_ref[...], query, NT, preferred_element_type=F32) + bias[...]
-    top = jnp.max(scores, axis=0, keepdims=True)
-    exp_scores = jnp.exp((scores - top) * scale)
-    total = jnp.sum(exp_scores, axis=0, keepdims=True)
-    weights = exp_scores * (1.0 / total)
-    weights_low = weights.astype(BF16)
-    grad_weights = lax.dot_general(value_ref[...], grad, NT, preferred_element_type=F32)
-    row_delta = jnp.sum(weights_low.astype(F32) * grad_weights, axis=0, keepdims=True)
-    grad_scores = (weights * (grad_weights - row_delta)).astype(BF16)
-    value_acc[...] += jnp.dot(weights_low, grad, preferred_element_type=F32)
-    key_acc[...] += jnp.dot(grad_scores, query, preferred_element_type=F32)
-
-    @pl.when(head == group - 1)
+    key, value = key_ref[...], value_ref[...]
+    heads = range(query_ref.shape[1] // HD)
+    cut = lambda ref: [ref[:, h * HD : (h + 1) * HD] for h in heads]
+    query, grad = cut(query_ref), cut(grad_ref)
+    scores = [lax.dot_general(key, query[h], NT, preferred_element_type=F32) + bias[...] for h in heads]
+    grad_weights = [lax.dot_general(value, grad[h], NT, preferred_element_type=F32) for h in heads]
+    key_part, value_part = key_acc[...], value_acc[...]
+    for h in heads:
+        top = jnp.max(scores[h], axis=0, keepdims=True)
+        exp_scores = jnp.exp2((scores[h] - top) * (scale * LOG2_E))
+        total = jnp.sum(exp_scores, axis=0, keepdims=True)
+        weights = exp_scores * (1.0 / total)
+        weights_low = weights.astype(BF16)
+        row_delta = jnp.sum(weights_low.astype(F32) * grad_weights[h], axis=0, keepdims=True)
+        grad_scores = (weights * (grad_weights[h] - row_delta)).astype(BF16)
+        value_part += jnp.dot(weights_low, grad[h], preferred_element_type=F32)
+        key_part += jnp.dot(grad_scores, query[h], preferred_element_type=F32)
+    key_acc[...] = key_part
+    value_acc[...] = value_part
+
+    @pl.when(head == pl.num_programs(0) - 1)
     def _():
         out_ref[:, :HD] = (key_acc[...] * scale).astype(BF16)
         out_ref[:, HD:] = value_acc[...].astype(BF16)
@@ -305,7 +314,6 @@
         limit=60,
         name="turn",
     )
-    turned[0], pairs = lax.optimization_barrier((turned[0], pairs))
     all_pairs = lax.all_gather(pairs, DP, axis=0, tiled=True)
     layers = [turned[0]] + [
         lax.ppermute(turned[d], "x", [(i, (i + d) % X_SIZE) for i in range(X_SIZE)]) for d in range(1, X_SIZE)
@@ -313,12 +321,13 @@
     arrived, *layers = lax.optimization_barrier((arrived, *layers))
     arrived = arrived.reshape(slots, -1)
 
-    column = lambda at: pl.BlockSpec((slots, HD), lambda h, at=at: (0, at + h))
+    steps = group // SERVER_HEADS
+    column = lambda at: pl.BlockSpec((slots, SERVER_HEADS * HD), lambda h, at=at: (0, at + h))
     fixed = lambda at: pl.BlockSpec((slots, HD), lambda h, at=at: (0, at))
     served = call(
-        functools.partial(server_kernel, group), [(slots, 2 * HD)], *[arrived] * 5,
-        grid=(group,),
-        in_specs=[fixed(2 * group + 2), column(0), column(group), fixed(2 * group), fixed(2 * group + 1)],
+        server_kernel, [(slots, 2 * HD)], *[arrived] * 5,
+        grid=(steps,),
+        in_specs=[fixed(2 * group + 2), column(0), column(steps), fixed(2 * group), fixed(2 * group + 1)],
         out_specs=[pl.BlockSpec((slots, 2 * HD), lambda h: (0, 0))],
         scratch_shapes=[pltpu.VMEM((slots, slots), F32), pltpu.VMEM((slots, HD), F32), pltpu.VMEM((slots, HD), F32)],
         name="server",

time: 275 us -> 268 us (0.975)
  waiting for transfers between devices: 134 us -> 130 us
    all_to_all x2, waiting for transfers between devices: 128 us -> 124 us  [swap(): return lax.all_to_all(block, axis, split_axis=0, concat_axis=0, tiled=True)]
where the time goes in v3:
time: 268 us
  waiting for transfers between devices  130 us (49%)
  blocking collectives  50.3 us (19%)
  starting transfers between devices  36.3 us (14%)
  Pallas kernels  31.4 us (12%)
  between operations  14.2 us (5%)
  local copies, waits for them, and re-layouts  3.03 us (1%)
    all_to_all x2, waiting for transfers between devices, swap(): return lax.all_to_all(block, axis, split_axis=0, concat_axis=0, tiled=True)  124 us
    all_to_all x2, blocking collectives, swap(): return lax.all_to_all(block, axis, split_axis=0, concat_axis=0, tiled=True)  50.3 us
    pallas_call x6, Pallas kernels, call(): pl.pallas_call(kernel, out_shape=shapes, in_specs=more.pop('in_specs', [w...  31.4 us
    all_to_all x2, starting transfers between devices, swap(): return lax.all_to_all(block, axis, split_axis=0, concat_axis=0, tiled=True)  22.8 us
    ppermute x3, starting transfers between devices, shards(): lax.ppermute(turned[d], 'x', [(i, (i + d) % X_SIZE) for i in range(X_SIZE)])  11.3 us
  transfers between devices with their start and end apart: 7, of which 5 were waited for; matrix products, arithmetic and copies ran while one was open for 2% of the time, Pallas kernels for 10%

profile of v3, /device:TPU:32, one launch (start us, length us, event | category | flops | bytes accessed | tf_op | source)
XLA Modules:
  0.0 267.6 jit_solution(7868467444975374557)
XLA Ops:
  7.2 4.1 %pack.1 = (bf16[512,2432]{1,0:T(8,128)(2,1)}, bf16[272,256]{1,0:T(8,128)(2,1)}, s32[8,256]{1,0:T(8,128)}) custom-call(s32[1,256]{1,0:T(1,128)} %bitcast.21, s32[1,256]{1,0:T(1,128)} %bitcast.22, s32[1,256]{1,0:T(1,128)} %bitcast.20, bf16[256,1024]{1,0:T(8,128)(2,1)} %query_hbm.3, bf16[256,1024]{1,0:T(8,128)(2,1)} %grad_hbm.3, bf16[256,128]{1,0:T(8,128)(2,1)} %key_hbm.1, ...), custom_call_target="tpu_custom_call" | custom-call | tf_op jit(solution)/shard_map/pack/pallas_call | solution.py:282
  11.3 18.2 %all-to-all-start = ((bf16[64,8,2432]{2,1,0:T(8,128)(2,1)}), bf16[64,8,2432]{2,1,0:T(8,128)(2,1)S(1)}, u32[]{:S(2)}, u32[]{:S(2)}) async-start(bf16[64,8,2432]{2,1,0:T(8,128)(2,1)} %bitcast.19), calls=%async_computation | async-start | bytes 4980736 | tf_op jit(solution)/shard_map/all_to_all | solution.py:293
  29.6 2.5 turn.1
  32.1 3.4 %collective-permute-start = (bf16[256,256]{1,0:T(8,128)(2,1)}, bf16[256,256]{1,0:T(8,128)(2,1)S(1)}, u32[]{:S(2)}, u32[]{:S(2)}) collective-permute-start(bf16[256,256]{1,0:T(8,128)(2,1)} %get-tuple-element.32), channel_id=1, source_target_pairs={{0,8},{8,16},{16,24},{24,0},{1,9},{9,17},{17,25},{25,1},{2,10},{10... | collective-permute-start | bytes 393224 | tf_op jit(solution)/shard_map/ppermute | solution.py:319
  35.4 4.6 %collective-permute-start.1 = (bf16[256,256]{1,0:T(8,128)(2,1)}, bf16[256,256]{1,0:T(8,128)(2,1)S(1)}, u32[]{:S(2)}, u32[]{:S(2)}) collective-permute-start(bf16[256,256]{1,0:T(8,128)(2,1)} %get-tuple-element.33), channel_id=1, source_target_pairs={{0,16},{8,24},{16,0},{24,8},{1,17},{9,25},{17,1},{25,9},{2,18},{10... | collective-permute-start | bytes 393224 | tf_op jit(solution)/shard_map/ppermute | solution.py:319
  40.0 3.4 %collective-permute-start.2 = (bf16[256,256]{1,0:T(8,128)(2,1)}, bf16[256,256]{1,0:T(8,128)(2,1)S(1)}, u32[]{:S(2)}, u32[]{:S(2)}) collective-permute-start(bf16[256,256]{1,0:T(8,128)(2,1)} %get-tuple-element.34), channel_id=1, source_target_pairs={{0,24},{8,0},{16,8},{24,16},{1,25},{9,1},{17,9},{25,17},{2,26},{10... | collective-permute-start | bytes 393224 | tf_op jit(solution)/shard_map/ppermute | solution.py:319
  43.4 3.6 %collective-permute-done.1.refs_2_ = bf16[256,256]{1,0:T(8,128)(2,1)S(1)} collective-permute-done((bf16[256,256]{1,0:T(8,128)(2,1)}, bf16[256,256]{1,0:T(8,128)(2,1)S(1)}, u32[]{:S(2)}, u32[]{:S(2)}) %collective-permute-start.1) | collective-permute-done | bytes 131104 | tf_op jit(solution)/shard_map/ppermute | solution.py:319
  47.2 112.3 %all-to-all-done = bf16[64,8,2432]{2,1,0:T(8,128)(2,1)S(1)} async-done(((bf16[64,8,2432]{2,1,0:T(8,128)(2,1)}), bf16[64,8,2432]{2,1,0:T(8,128)(2,1)S(1)}, u32[]{:S(2)}, u32[]{:S(2)}) %all-to-all-start) | async-done | bytes 2490400 | tf_op jit(solution)/shard_map/all_to_all | solution.py:293
  159.5 7.9 %server.1 = bf16[512,256]{1,0:T(8,128)(2,1)S(1)} custom-call(bf16[512,2432]{1,0:T(8,128)(2,1)S(1)} %bitcast.11, bf16[512,2432]{1,0:T(8,128)(2,1)S(1)} %bitcast.12, bf16[512,2432]{1,0:T(8,128)(2,1)S(1)} %bitcast.13, bf16[512,2432]{1,0:T(8,128)(2,1)S(1)} %bitcast.14, bf16[512,2432]{1,0:T(8,128)(2,1)S(1)} %bitcast.15), custom_call_target="tpu_custom_call" | custom-call | tf_op jit(solution)/shard_map/server/pallas_call | solution.py:282
  167.4 30.4 %all_to_all.20 = bf16[64,8,256]{2,1,0:T(8,128)(2,1)S(1)} all-to-all(bf16[64,8,256]{2,1,0:T(8,128)(2,1)S(1)} %bitcast.16), channel_id=1, replica_groups=mesh['zh'=4,'zl'=4,'x'=4,'y'=4,'c'=2] {'zh','zl','x'}, dimensions={0} | all-to-all | bytes 524288 | tf_op jit(solution)/shard_map/all_to_all | solution.py:293
  197.8 1.0 own.1
  198.7 19.9 %all_to_all.21.refs_4_ = bf16[16,256,128]{2,1,0:T(8,128)(2,1)S(1)} all-to-all(bf16[16,256,128]{2,1,0:T(8,128)(2,1)S(1)} %get-tuple-element.41), channel_id=1, replica_groups=mesh['zh'=4,'zl'=4,'x'=4,'y'=4,'c'=2] {'x','y'}, dimensions={0} | all-to-all | bytes 2097152 | tf_op jit(solution)/shard_map/all_to_all | solution.py:293
  218.7 2.0 collective-permute-start.3
  220.7 2.6 collective-permute-done.3.refs_5_
  223.3 2.1 weight.1
  225.4 4.6 %all-to-all-start.3 = ((bf16[16,16,1024]{2,1,0:T(8,128)(2,1)}), bf16[16,16,1024]{2,1,0:T(8,128)(2,1)S(1)}, u32[]{:S(2)}, u32[]{:S(2)}) async-start(bf16[16,16,1024]{2,1,0:T(8,128)(2,1)} %bitcast.10), calls=%async_computation.3 | async-start | bytes 1048576 | tf_op jit(solution)/shard_map/all_to_all | solution.py:293
  230.3 0.6 and_select_fusion.reach_ref
  230.9 2.4 slice.17
  233.3 0.2 slice_reduce_fusion.1
  233.7 0.3 fusion.1
  234.0 0.9 fusion.place_ref
  234.9 13.9 %home.1 = (bf16[256,1024]{1,0:T(8,128)(2,1)}, bf16[256,1024]{1,0:T(8,128)(2,1)}) custom-call(s32[32,64]{1,0:T(8,128)} %fusion.place_ref, s32[32]{0:T(128)} %and_select_fusion.reach_ref, bf16[256,1024]{1,0:T(8,128)(2,1)} %query_hbm.3, bf16[256,1024]{1,0:T(8,128)(2,1)} %grad_hbm.3, bf16[17408,256]{1,0:T(8,128)(2,1)} %all-gather.2.cloned.1.call-done.pairs_ref), custom_call_target="tpu_custom_call" | custom-call | tf_op jit(solution)/shard_map/home/pallas_call | solution.py:282
  248.8 11.2 %all-to-all-done.3 = bf16[16,16,1024]{2,1,0:T(8,128)(2,1)S(1)} async-done(((bf16[16,16,1024]{2,1,0:T(8,128)(2,1)}), bf16[16,16,1024]{2,1,0:T(8,128)(2,1)S(1)}, u32[]{:S(2)}, u32[]{:S(2)}) %all-to-all-start.3) | async-done | bytes 524320 | tf_op jit(solution)/shard_map/all_to_all | solution.py:293
  260.1 0.6 broadcast_multiply_fusion
  (22 shorter events, 0.7 us)
Async XLA Ops:
  7.2 218.2 %all-gather.2.cloned.1.call-start = ((), (), s32[]{:S(2)}) async-start(), calls=%async_computation.4 | async-start | bytes 9052160 | tf_op jit(solution)/shard_map/all_gather | solution.py:317
  11.3 148.1 %all-to-all-start = ((bf16[64,8,2432]{2,1,0:T(8,128)(2,1)}), bf16[64,8,2432]{2,1,0:T(8,128)(2,1)S(1)}, u32[]{:S(2)}, u32[]{:S(2)}) async-start(bf16[64,8,2432]{2,1,0:T(8,128)(2,1)} %bitcast.19), calls=%async_computation | async-start | bytes 4980736 | tf_op jit(solution)/shard_map/all_to_all | solution.py:293
  32.1 11.4 %collective-permute-start = (bf16[256,256]{1,0:T(8,128)(2,1)}, bf16[256,256]{1,0:T(8,128)(2,1)S(1)}, u32[]{:S(2)}, u32[]{:S(2)}) collective-permute-start(bf16[256,256]{1,0:T(8,128)(2,1)} %get-tuple-element.32), channel_id=1, source_target_pairs={{0,8},{8,16},{16,24},{24,0},{1,9},{9,17},{17,25},{25,1},{2,10},{10... | collective-permute-start | bytes 393224 | tf_op jit(solution)/shard_map/ppermute | solution.py:319
  35.4 11.6 %collective-permute-start.1 = (bf16[256,256]{1,0:T(8,128)(2,1)}, bf16[256,256]{1,0:T(8,128)(2,1)S(1)}, u32[]{:S(2)}, u32[]{:S(2)}) collective-permute-start(bf16[256,256]{1,0:T(8,128)(2,1)} %get-tuple-element.33), channel_id=1, source_target_pairs={{0,16},{8,24},{16,0},{24,8},{1,17},{9,25},{17,1},{25,9},{2,18},{10... | collective-permute-start | bytes 393224 | tf_op jit(solution)/shard_map/ppermute | solution.py:319
  40.0 7.1 %collective-permute-start.2 = (bf16[256,256]{1,0:T(8,128)(2,1)}, bf16[256,256]{1,0:T(8,128)(2,1)S(1)}, u32[]{:S(2)}, u32[]{:S(2)}) collective-permute-start(bf16[256,256]{1,0:T(8,128)(2,1)} %get-tuple-element.34), channel_id=1, source_target_pairs={{0,24},{8,0},{16,8},{24,16},{1,25},{9,1},{17,9},{25,17},{2,26},{10... | collective-permute-start | bytes 393224 | tf_op jit(solution)/shard_map/ppermute | solution.py:319
  159.5 38.3 %copy-start.1 = (s32[8,256]{1,0:T(8,128)S(1)}, s32[8,256]{1,0:T(8,128)}, u32[]{:S(2)}) copy-start(s32[8,256]{1,0:T(8,128)} %get-tuple-element.39.slot_ref) | copy-start | bytes 24580
  167.4 56.0 %copy-start = (bf16[256,256]{1,0:T(8,128)(2,1)S(1)}, bf16[256,256]{1,0:T(8,128)(2,1)}, u32[]{:S(2)}) copy-start(bf16[256,256]{1,0:T(8,128)(2,1)} %get-tuple-element.35.refs_0_) | copy-start | bytes 393220
  218.7 11.4 %copy-start.2 = (s32[256]{0:T(256)S(1)}, s32[256]{0:T(256)}, u32[]{:S(2)}) copy-start(s32[256]{0:T(256)} %param.13) | copy-start | bytes 3076
  218.7 11.4 %copy-start.3 = (s32[256]{0:T(256)S(1)}, s32[256]{0:T(256)}, u32[]{:S(2)}) copy-start(s32[256]{0:T(256)} %param.14) | copy-start | bytes 3076
  218.7 4.7 %collective-permute-start.3 = (bf16[16,256,128]{2,1,0:T(8,128)(2,1)S(1)}, bf16[16,256,128]{2,1,0:T(8,128)(2,1)S(1)}, u32[]{:S(2)}, u32[]{:S(2)}) collective-permute-start(bf16[16,256,128]{2,1,0:T(8,128)(2,1)S(1)} %all_to_all.21.refs_4_), channel_id=1, source_target_pairs={{0,1},{1,0},{2,3},{3,2},{4,5},{5,4},{6,7},{7,6},{8,9},{9,8},{10,11... | collective-permute-start | bytes 3145736 | tf_op jit(solution)/shard_map/ppermute | solution.py:343
  225.4 34.6 %all-to-all-start.3 = ((bf16[16,16,1024]{2,1,0:T(8,128)(2,1)}), bf16[16,16,1024]{2,1,0:T(8,128)(2,1)S(1)}, u32[]{:S(2)}, u32[]{:S(2)}) async-start(bf16[16,16,1024]{2,1,0:T(8,128)(2,1)} %bitcast.10), calls=%async_computation.3 | async-start | bytes 1048576 | tf_op jit(solution)/shard_map/all_to_all | solution.py:293
Sparse Core Ops, SparseCore 0:
  11.5 209.5 all-gather.1

commit v4 on v3

--- a/solution.py
+++ b/solution.py
@@ -16,6 +16,7 @@
 MAX_RUNS = 64
 STEP_RUNS = 16
 BRING = 4
+PACK_COLUMNS = 1024
 LOG2_E = math.log2(math.e)
 SERVER_HEADS = 4
 TAG_ROWS = 16
@@ -79,10 +80,13 @@
     for copy, ref in zip(arrivals[3:], targets[3:]):
         copy.wait()
         width = ref.shape[1]
-        out_ref[:, at : at + width] = jnp.dot(hot, ref[...], preferred_element_type=F32).astype(BF16)
-        at += width
-        if width > HD:
-            send(at - width, at)
+        part = min(width, PACK_COLUMNS)
+        for begin in range(0, width, part):
+            rows = jnp.dot(hot, ref[:, begin : begin + part], preferred_element_type=F32).astype(BF16)
+            out_ref[:, at : at + part] = rows
+            at += part
+            if width > HD:
+                send(at - part, at)
     out_ref[:, at : at + HD] = tags
     send(at - 2 * HD, at + HD)
     pairs_ref[:tokens, :HD] = key_ref[...]
@@ -252,13 +256,15 @@
     layers, own_ref, other_ref, out_ref = refs[:X_SIZE], refs[X_SIZE], refs[X_SIZE + 1], refs[X_SIZE + 2]
     me, core = x_ref[0], core_ref[0]
     y_size = own_ref.shape[0] // X_SIZE
+    layer = jnp.concatenate([ref[...] for ref in layers], axis=1)
     for y in range(y_size):
-        for grads, c in ((own_ref, core), (other_ref, 1 - core)):
-            total = jnp.dot(layers[0][...], grads[me * y_size + y], preferred_element_type=F32)
-            for d in range(1, X_SIZE):
-                there = (me - d + X_SIZE) % X_SIZE
-                total += jnp.dot(layers[d][...], grads[there * y_size + y], preferred_element_type=F32)
-            out_ref[:, pl.ds(pl.multiple_of((2 * y + c) * HD, HD), HD)] = total.astype(BF16)
+        parts = []
+        for d in range(X_SIZE):
+            at = (me - d + X_SIZE) % X_SIZE * y_size + y
+            own, other = own_ref[at], other_ref[at]
+            parts.append(jnp.concatenate([jnp.where(core == 0, own, other), jnp.where(core == 0, other, own)], axis=1))
+        total = jnp.dot(layer, jnp.concatenate(parts, axis=0), preferred_element_type=F32)
+        out_ref[:, 2 * y * HD : 2 * (y + 1) * HD] = total.astype(BF16)
 
 
 def exact_pick(left, right):
@@ -300,7 +306,7 @@
         out_specs=[whole(pltpu.HBM), whole(), whole()],
         scratch_shapes=[pltpu.VMEM((1, tokens), jnp.int32)] * 2 + [pltpu.VMEM(servers.shape, jnp.int32)]
         + [pltpu.VMEM((tokens, width), BF16)] * 2 + [pltpu.VMEM((tokens, HD), BF16)] * 2
-        + [pltpu.VMEM((slots, 2 * width + 3 * HD), BF16), pltpu.SemaphoreType.DMA((7,)), pltpu.SemaphoreType.DMA((3,))],
+        + [pltpu.VMEM((slots, 2 * width + 3 * HD), BF16), pltpu.SemaphoreType.DMA((7,)), pltpu.SemaphoreType.DMA((2 * width // PACK_COLUMNS + 1,))],
         limit=60,
         name="pack",
     )

time: 268 us -> 268 us (level)
  no operation moved by 1% of the time
where the time goes in v4:
time: 268 us; the launch traced here: 267 us
  waiting for transfers between devices  130 us (49%)
  blocking collectives  50.3 us (19%)
  starting transfers between devices  36.3 us (14%)
  Pallas kernels  30.7 us (11%)
  between operations  14.2 us (5%)
  local copies, waits for them, and re-layouts  3.03 us (1%)
    all_to_all x2, waiting for transfers between devices, swap(): return lax.all_to_all(block, axis, split_axis=0, concat_axis=0, tiled=True)  124 us
    all_to_all x2, blocking collectives, swap(): return lax.all_to_all(block, axis, split_axis=0, concat_axis=0, tiled=True)  50.3 us
    pallas_call x6, Pallas kernels, call(): pl.pallas_call(kernel, out_shape=shapes, in_specs=more.pop('in_specs', [w...  30.7 us
    all_to_all x2, starting transfers between devices, swap(): return lax.all_to_all(block, axis, split_axis=0, concat_axis=0, tiled=True)  22.8 us
    ppermute x3, starting transfers between devices, shards(): lax.ppermute(turned[d], 'x', [(i, (i + d) % X_SIZE) for i in range(X_SIZE)])  11.3 us
  transfers between devices with their start and end apart: 7, of which 5 were waited for; matrix products, arithmetic and copies ran while one was open for 2% of the time, Pallas kernels for 10%

profile of v4, /device:TPU:32, one launch (start us, length us, event | category | flops | bytes accessed | tf_op | source)
XLA Modules:
  0.0 267.1 jit_solution(18101992035217307198)
XLA Ops:
  7.2 4.1 %pack.1 = (bf16[512,2432]{1,0:T(8,128)(2,1)}, bf16[272,256]{1,0:T(8,128)(2,1)}, s32[8,256]{1,0:T(8,128)}) custom-call(s32[1,256]{1,0:T(1,128)} %bitcast.21, s32[1,256]{1,0:T(1,128)} %bitcast.22, s32[1,256]{1,0:T(1,128)} %bitcast.20, bf16[256,1024]{1,0:T(8,128)(2,1)} %query_hbm.3, bf16[256,1024]{1,0:T(8,128)(2,1)} %grad_hbm.3, bf16[256,128]{1,0:T(8,128)(2,1)} %key_hbm.1, ...), custom_call_target="tpu_custom_call" | custom-call | tf_op jit(solution)/shard_map/pack/pallas_call | solution.py:288
  11.3 18.2 %all-to-all-start = ((bf16[64,8,2432]{2,1,0:T(8,128)(2,1)}), bf16[64,8,2432]{2,1,0:T(8,128)(2,1)S(1)}, u32[]{:S(2)}, u32[]{:S(2)}) async-start(bf16[64,8,2432]{2,1,0:T(8,128)(2,1)} %bitcast.19), calls=%async_computation | async-start | bytes 4980736 | tf_op jit(solution)/shard_map/all_to_all | solution.py:299
  29.6 2.5 turn.1
  32.1 3.4 %collective-permute-start = (bf16[256,256]{1,0:T(8,128)(2,1)}, bf16[256,256]{1,0:T(8,128)(2,1)S(1)}, u32[]{:S(2)}, u32[]{:S(2)}) collective-permute-start(bf16[256,256]{1,0:T(8,128)(2,1)} %get-tuple-element.32), channel_id=1, source_target_pairs={{0,8},{8,16},{16,24},{24,0},{1,9},{9,17},{17,25},{25,1},{2,10},{10... | collective-permute-start | bytes 393224 | tf_op jit(solution)/shard_map/ppermute | solution.py:325
  35.4 4.6 %collective-permute-start.1 = (bf16[256,256]{1,0:T(8,128)(2,1)}, bf16[256,256]{1,0:T(8,128)(2,1)S(1)}, u32[]{:S(2)}, u32[]{:S(2)}) collective-permute-start(bf16[256,256]{1,0:T(8,128)(2,1)} %get-tuple-element.33), channel_id=1, source_target_pairs={{0,16},{8,24},{16,0},{24,8},{1,17},{9,25},{17,1},{25,9},{2,18},{10... | collective-permute-start | bytes 393224 | tf_op jit(solution)/shard_map/ppermute | solution.py:325
  40.0 3.4 %collective-permute-start.2 = (bf16[256,256]{1,0:T(8,128)(2,1)}, bf16[256,256]{1,0:T(8,128)(2,1)S(1)}, u32[]{:S(2)}, u32[]{:S(2)}) collective-permute-start(bf16[256,256]{1,0:T(8,128)(2,1)} %get-tuple-element.34), channel_id=1, source_target_pairs={{0,24},{8,0},{16,8},{24,16},{1,25},{9,1},{17,9},{25,17},{2,26},{10... | collective-permute-start | bytes 393224 | tf_op jit(solution)/shard_map/ppermute | solution.py:325
  43.4 3.6 %collective-permute-done.1.refs_2_ = bf16[256,256]{1,0:T(8,128)(2,1)S(1)} collective-permute-done((bf16[256,256]{1,0:T(8,128)(2,1)}, bf16[256,256]{1,0:T(8,128)(2,1)S(1)}, u32[]{:S(2)}, u32[]{:S(2)}) %collective-permute-start.1) | collective-permute-done | bytes 131104 | tf_op jit(solution)/shard_map/ppermute | solution.py:325
  47.2 112.3 %all-to-all-done = bf16[64,8,2432]{2,1,0:T(8,128)(2,1)S(1)} async-done(((bf16[64,8,2432]{2,1,0:T(8,128)(2,1)}), bf16[64,8,2432]{2,1,0:T(8,128)(2,1)S(1)}, u32[]{:S(2)}, u32[]{:S(2)}) %all-to-all-start) | async-done | bytes 2490400 | tf_op jit(solution)/shard_map/all_to_all | solution.py:299
  159.5 7.9 %server.1 = bf16[512,256]{1,0:T(8,128)(2,1)S(1)} custom-call(bf16[512,2432]{1,0:T(8,128)(2,1)S(1)} %bitcast.11, bf16[512,2432]{1,0:T(8,128)(2,1)S(1)} %bitcast.12, bf16[512,2432]{1,0:T(8,128)(2,1)S(1)} %bitcast.13, bf16[512,2432]{1,0:T(8,128)(2,1)S(1)} %bitcast.14, bf16[512,2432]{1,0:T(8,128)(2,1)S(1)} %bitcast.15), custom_call_target="tpu_custom_call" | custom-call | tf_op jit(solution)/shard_map/server/pallas_call | solution.py:288
  167.4 30.4 %all_to_all.20 = bf16[64,8,256]{2,1,0:T(8,128)(2,1)S(1)} all-to-all(bf16[64,8,256]{2,1,0:T(8,128)(2,1)S(1)} %bitcast.16), channel_id=1, replica_groups=mesh['zh'=4,'zl'=4,'x'=4,'y'=4,'c'=2] {'zh','zl','x'}, dimensions={0} | all-to-all | bytes 524288 | tf_op jit(solution)/shard_map/all_to_all | solution.py:299
  197.8 1.0 own.1
  198.7 19.9 %all_to_all.21.refs_4_ = bf16[16,256,128]{2,1,0:T(8,128)(2,1)S(1)} all-to-all(bf16[16,256,128]{2,1,0:T(8,128)(2,1)S(1)} %get-tuple-element.41), channel_id=1, replica_groups=mesh['zh'=4,'zl'=4,'x'=4,'y'=4,'c'=2] {'x','y'}, dimensions={0} | all-to-all | bytes 2097152 | tf_op jit(solution)/shard_map/all_to_all | solution.py:299
  218.7 2.0 collective-permute-start.3
  220.7 2.6 collective-permute-done.3.refs_5_
  223.3 1.6 weight.1
  224.9 4.6 %all-to-all-start.3 = ((bf16[16,16,1024]{2,1,0:T(8,128)(2,1)}), bf16[16,16,1024]{2,1,0:T(8,128)(2,1)S(1)}, u32[]{:S(2)}, u32[]{:S(2)}) async-start(bf16[16,16,1024]{2,1,0:T(8,128)(2,1)} %bitcast.10), calls=%async_computation.3 | async-start | bytes 1048576 | tf_op jit(solution)/shard_map/all_to_all | solution.py:299
  229.8 0.6 and_select_fusion.reach_ref
  230.4 2.4 slice.17
  232.8 0.2 slice_reduce_fusion.1
  233.2 0.3 fusion.1
  233.5 0.9 fusion.place_ref
  234.3 13.7 %home.1 = (bf16[256,1024]{1,0:T(8,128)(2,1)}, bf16[256,1024]{1,0:T(8,128)(2,1)}) custom-call(s32[32,64]{1,0:T(8,128)} %fusion.place_ref, s32[32]{0:T(128)} %and_select_fusion.reach_ref, bf16[256,1024]{1,0:T(8,128)(2,1)} %query_hbm.3, bf16[256,1024]{1,0:T(8,128)(2,1)} %grad_hbm.3, bf16[17408,256]{1,0:T(8,128)(2,1)} %all-gather.2.cloned.1.call-done.pairs_ref), custom_call_target="tpu_custom_call" | custom-call | tf_op jit(solution)/shard_map/home/pallas_call | solution.py:288
  248.0 11.5 %all-to-all-done.3 = bf16[16,16,1024]{2,1,0:T(8,128)(2,1)S(1)} async-done(((bf16[16,16,1024]{2,1,0:T(8,128)(2,1)}), bf16[16,16,1024]{2,1,0:T(8,128)(2,1)S(1)}, u32[]{:S(2)}, u32[]{:S(2)}) %all-to-all-start.3) | async-done | bytes 524320 | tf_op jit(solution)/shard_map/all_to_all | solution.py:299
  259.6 0.6 broadcast_multiply_fusion
  (22 shorter events, 0.7 us)
Async XLA Ops:
  7.2 217.7 %all-gather.2.cloned.1.call-start = ((), (), s32[]{:S(2)}) async-start(), calls=%async_computation.4 | async-start | bytes 9052160 | tf_op jit(solution)/shard_map/all_gather | solution.py:323
  11.3 148.1 %all-to-all-start = ((bf16[64,8,2432]{2,1,0:T(8,128)(2,1)}), bf16[64,8,2432]{2,1,0:T(8,128)(2,1)S(1)}, u32[]{:S(2)}, u32[]{:S(2)}) async-start(bf16[64,8,2432]{2,1,0:T(8,128)(2,1)} %bitcast.19), calls=%async_computation | async-start | bytes 4980736 | tf_op jit(solution)/shard_map/all_to_all | solution.py:299
  32.1 11.4 %collective-permute-start = (bf16[256,256]{1,0:T(8,128)(2,1)}, bf16[256,256]{1,0:T(8,128)(2,1)S(1)}, u32[]{:S(2)}, u32[]{:S(2)}) collective-permute-start(bf16[256,256]{1,0:T(8,128)(2,1)} %get-tuple-element.32), channel_id=1, source_target_pairs={{0,8},{8,16},{16,24},{24,0},{1,9},{9,17},{17,25},{25,1},{2,10},{10... | collective-permute-start | bytes 393224 | tf_op jit(solution)/shard_map/ppermute | solution.py:325
  35.4 11.6 %collective-permute-start.1 = (bf16[256,256]{1,0:T(8,128)(2,1)}, bf16[256,256]{1,0:T(8,128)(2,1)S(1)}, u32[]{:S(2)}, u32[]{:S(2)}) collective-permute-start(bf16[256,256]{1,0:T(8,128)(2,1)} %get-tuple-element.33), channel_id=1, source_target_pairs={{0,16},{8,24},{16,0},{24,8},{1,17},{9,25},{17,1},{25,9},{2,18},{10... | collective-permute-start | bytes 393224 | tf_op jit(solution)/shard_map/ppermute | solution.py:325
  40.0 7.1 %collective-permute-start.2 = (bf16[256,256]{1,0:T(8,128)(2,1)}, bf16[256,256]{1,0:T(8,128)(2,1)S(1)}, u32[]{:S(2)}, u32[]{:S(2)}) collective-permute-start(bf16[256,256]{1,0:T(8,128)(2,1)} %get-tuple-element.34), channel_id=1, source_target_pairs={{0,24},{8,0},{16,8},{24,16},{1,25},{9,1},{17,9},{25,17},{2,26},{10... | collective-permute-start | bytes 393224 | tf_op jit(solution)/shard_map/ppermute | solution.py:325
  159.5 38.3 %copy-start.1 = (s32[8,256]{1,0:T(8,128)S(1)}, s32[8,256]{1,0:T(8,128)}, u32[]{:S(2)}) copy-start(s32[8,256]{1,0:T(8,128)} %get-tuple-element.39.slot_ref) | copy-start | bytes 24580
  167.4 56.0 %copy-start = (bf16[256,256]{1,0:T(8,128)(2,1)S(1)}, bf16[256,256]{1,0:T(8,128)(2,1)}, u32[]{:S(2)}) copy-start(bf16[256,256]{1,0:T(8,128)(2,1)} %get-tuple-element.35.refs_0_) | copy-start | bytes 393220
  218.7 10.9 %copy-start.2 = (s32[256]{0:T(256)S(1)}, s32[256]{0:T(256)}, u32[]{:S(2)}) copy-start(s32[256]{0:T(256)} %param.13) | copy-start | bytes 3076
  218.7 10.9 %copy-start.3 = (s32[256]{0:T(256)S(1)}, s32[256]{0:T(256)}, u32[]{:S(2)}) copy-start(s32[256]{0:T(256)} %param.14) | copy-start | bytes 3076
  218.7 4.7 %collective-permute-start.3 = (bf16[16,256,128]{2,1,0:T(8,128)(2,1)S(1)}, bf16[16,256,128]{2,1,0:T(8,128)(2,1)S(1)}, u32[]{:S(2)}, u32[]{:S(2)}) collective-permute-start(bf16[16,256,128]{2,1,0:T(8,128)(2,1)S(1)} %all_to_all.21.refs_4_), channel_id=1, source_target_pairs={{0,1},{1,0},{2,3},{3,2},{4,5},{5,4},{6,7},{7,6},{8,9},{9,8},{10,11... | collective-permute-start | bytes 3145736 | tf_op jit(solution)/shard_map/ppermute | solution.py:349
  224.9 34.6 %all-to-all-start.3 = ((bf16[16,16,1024]{2,1,0:T(8,128)(2,1)}), bf16[16,16,1024]{2,1,0:T(8,128)(2,1)S(1)}, u32[]{:S(2)}, u32[]{:S(2)}) async-start(bf16[16,16,1024]{2,1,0:T(8,128)(2,1)} %bitcast.10), calls=%async_computation.3 | async-start | bytes 1048576 | tf_op jit(solution)/shard_map/all_to_all | solution.py:299
Sparse Core Ops, SparseCore 0:
  11.5 209.5 all-gather.1
